TPU v7x, 512 devices: a whole 4x8x8 slice. The times are simulated.
512 devices in a mesh: span: 32 (over y_lo, z, core), wrap: 4 (over y_hi), normal: 4 (over x).
Axes of the slice: x: 4, y: 8 (y_hi: 4, y_lo: 2; y = y_hi * 2 + y_lo), z: 8, core: 2. Of those that a mesh axis runs over, the one named last changes fastest.
Arguments:
- flow_state: float32 [5, 256, 64, 512], P(None, 'span', 'wrap', 'normal'), may hold values from -6 to 6
- inv_volume: float32 [256, 64, 512], P('span', 'wrap', 'normal'), may hold values from 0.5 to 2
- flux_jacobians: float32 [3, 5, 5], replicated, may hold values from -2.5 to 2.5
- area: float32 [256, 64], P('span', 'wrap'), may hold values from 0.5 to 2
- station_map: int32 [256, 64], P('span', 'wrap'), may hold values from 0 to 127, as said below
- contact: int32 [128], replicated, may hold values from 0 to 2
- bending: float32 [128], replicated, may hold values from 50 to 400
- mass: float32 [128], replicated, may hold values from 0.25 to 1.75
- hardening: float32 [128], replicated, may hold values from 2 to 12
- disp_old: float32 [128], replicated, may hold values from -2 to 2
- vel_old: float32 [128], replicated, may hold values from -6 to 6
Outputs:
- flow_next: float32 [5, 256, 64, 512], P(None, 'span', 'wrap', 'normal')
- deflection: float32 [128], replicated
Inputs may be any that keep to these rules, and one draw needn't show every extreme that they name: `station_map`: each face's station differs by at most one from floor(i * 128 / 256) for its span index i.
All inputs are finite; a program needn't handle non-finite values.
Results may differ from a plain program's by a relative error of at most 0.0001.
Values sent between devices are 32-bit elements; how exact they have to be, the bound alone decides.
A program may use at most 64 MiB of HBM per device.

v0:
```python
import functools

import jax
import jax.numpy as jnp
from jax import lax
from jax.experimental import pallas as pl
from jax.experimental.pallas import tpu as pltpu
from jax.sharding import PartitionSpec as P

MESH = pl.DeviceIdType.MESH
VARS = 5
STATIONS = 128
NEWTON = 3
DT_FLOW = 0.2
DISSIPATION = 0.03
DT_BEAM = 0.2
STOP_GAP = 0.5
CONTACT_STIFF = 40.0
SPAN, WRAP, LANES = 8, 16, 128
TOP = 8


def lane_of(shape):
    return lax.broadcasted_iota(jnp.int32, shape, len(shape) - 1)


def roll(x, shift):
    return pltpu.roll(x, shift % LANES if isinstance(shift, int) else shift, 1)


def factor(be, bo, diag_e, diag_o):
    lane = lane_of((1, LANES))
    half = LANES // 2
    valid, inner = lane < half, lane < half - 1
    bo_prev, be_next = roll(bo, 1), roll(be, -1)
    p = jnp.where(valid, 4.0 * be + bo_prev + bo + diag_e, 1.0)
    q = jnp.where(valid, -2.0 * (be + bo), 0.0)
    r = jnp.where(valid, 4.0 * bo + be + be_next + diag_o, 1.0)
    c11 = jnp.where(inner, bo, 0.0)
    c12 = jnp.zeros_like(bo)
    c21 = jnp.where(inner, -2.0 * (bo + be_next), 0.0)
    c22 = jnp.where(inner, be_next, 0.0)
    a11, a12, a21, a22 = roll(c11, 1), roll(c21, 1), c12, roll(c22, 1)
    levels = []
    step = 1
    while step < half:
        inv = 1.0 / (p * r - q * q)
        w11, w12, w22 = r * inv, -q * inv, p * inv
        u11, u12 = c11 * w11 + c21 * w12, c11 * w12 + c21 * w22
        u21, u22 = c12 * w11 + c22 * w12, c12 * w12 + c22 * w22
        d11, d12 = a11 * w11 + a21 * w12, a11 * w12 + a21 * w22
        d21, d22 = a12 * w11 + a22 * w12, a12 * w12 + a22 * w22
        levels.append((step, u11, u12, u21, u22, d11, d12, d21, d22))
        p = p - roll(u11 * c11 + u12 * c21, step) - roll(d11 * a11 + d12 * a21, -step)
        q = q - roll(u11 * c12 + u12 * c22, step) - roll(d11 * a12 + d12 * a22, -step)
        r = r - roll(u21 * c12 + u22 * c22, step) - roll(d21 * a12 + d22 * a22, -step)
        if 2 * step < half:
            n11, n12 = -(d11 * c11 + d12 * c21), -(d11 * c12 + d12 * c22)
            n21, n22 = -(d21 * c11 + d22 * c21), -(d21 * c12 + d22 * c22)
            c11, c12 = roll(n11, -step), roll(n12, -step)
            c21, c22 = roll(n21, -step), roll(n22, -step)
            a11, a12 = roll(n11, step), roll(n21, step)
            a21, a22 = roll(n12, step), roll(n22, step)
        step *= 2
    inv = 1.0 / (p * r - q * q)
    return levels, (r * inv, -q * inv, p * inv)


def substitute(factors, e, o):
    levels, (w11, w12, w22) = factors
    for step, u11, u12, u21, u22, d11, d12, d21, d22 in levels:
        e, o = (
            e - roll(u11 * e + u12 * o, step) - roll(d11 * e + d12 * o, -step),
            o - roll(u21 * e + u22 * o, step) - roll(d21 * e + d22 * o, -step),
        )
    return w11 * e + w12 * o, w12 * e + w22 * o


def right_side(fe, fo, he, ho, ue, uo):
    return fe + 2.0 * he * ue * ue * ue, fo + 2.0 * ho * uo * uo * uo


def halves(x):
    valid = lane_of((1, LANES)) < LANES // 2
    return jnp.where(valid, x, 0.0), jnp.where(valid, roll(x, LANES // 2), 0.0)


def pack_plane(packed, cells, s):
    slot = lane_of((8, LANES)) // 4
    new = []
    for v in range(VARS):
        have = packed[v]
        for t in range(2):
            k = 2 * s + t
            have = jnp.where(slot == k, roll(cells[v][t], 4 * k + 2), have)
        new.append(have)
    return tuple(new)


def edge_terms(normal, n_norm, own, left, right, jac, corr):
    lane = lane_of((8, LANES))
    place = lane % 4
    ends, smooths = [], []
    for v in range(VARS):
        mine = own[v]
        mirror = jnp.where(place == 0, roll(mine, -3), roll(mine, -1))
        low = jnp.where(normal == 0, mirror, left[v])
        high = jnp.where(normal == n_norm - 1, 0.0, right[v])
        delta = jnp.where(place < 2, roll(high - mine, -2), roll(low - mine, 2))
        near = jnp.where(place == 1, roll(delta, 1), jnp.where(place == 2, roll(delta, -1), 0.0))
        end = delta - 8.0 * near
        ends.append(jnp.where(place < 2, -end, end))
        smooths.append(delta - 4.0 * near)
    for u in range(VARS):
        total = -DISSIPATION * smooths[u]
        for v in range(VARS):
            total = total + jac[50 + 5 * u + v] * ends[v]
        corr[u] = total


def plane_rates(field, s, jac, corr):
    lane = lane_of((8, LANES))
    edge = (lane < 2) | (lane >= LANES - 2)
    cells, grads, smooths = [], [[], [], []], []
    for v in range(VARS):

        def at(ds, dw):
            return field[v, s + (2 + ds), TOP + dw : TOP + dw + WRAP, :]

        c = at(0, 0)
        reads = [
            [at(k, 0) for k in (-2, -1, 1, 2)],
            [at(0, k) for k in (-2, -1, 1, 2)],
            [roll(c, -k) for k in (-2, -1, 1, 2)],
        ]
        near, far = None, None
        for d, (m2, m1, p1, p2) in enumerate(reads):
            grads[d].append(((m2 - p2) + 8.0 * (p1 - m1)).reshape(2, 8, LANES))
            near = (m1 + p1) if near is None else near + (m1 + p1)
            far = (m2 + p2) if far is None else far + (m2 + p2)
        smooths.append((-DISSIPATION * (far - 4.0 * near + 18.0 * c)).reshape(2, 8, LANES))
        cells.append(c.reshape(2, 8, LANES))
    rates = []
    for u in range(VARS):
        total = smooths[u]
        for d in range(3):
            for v in range(VARS):
                total = total + jac[25 * d + 5 * u + v][None] * grads[d][v]
        ends = corr[u]
        fix = [
            jnp.where(edge, roll(ends, (2 * LANES - 2 - 4 * (2 * s + t)) % LANES), 0.0)
            for t in range(2)
        ]
        rates.append(total + jnp.stack(fix))
    return cells, rates


def kernel(
    n_span,
    n_wrap,
    n_norm,
    flow_hbm,
    volume_hbm,
    jac_smem,
    area_hbm,
    map_hbm,
    contact_hbm,
    bending_hbm,
    mass_hbm,
    hardening_hbm,
    disp_hbm,
    vel_hbm,
    out_hbm,
    state_ref,
    field1,
    field2,
    volume,
    wall_send,
    wall_recv,
    edges,
    corr,
    jac,
    result,
    faces,
    area,
    stations,
    contact_v,
    beam_v,
    loads_a,
    loads_b,
    tally,
    local_sem,
    send_sem,
    recv_sem,
    group_sem,
):
    span, wrap, normal = lax.axis_index("span"), lax.axis_index("wrap"), lax.axis_index("normal")
    rows = 2
    cols = n_span // rows
    row, col = span // cols, span % cols

    inputs = [
        (flow_hbm, field1.at[:, 2 : 2 + SPAN, TOP : TOP + WRAP, :]),
        (volume_hbm, volume),
        (area_hbm, area),
        (map_hbm, stations),
        (contact_hbm, contact_v),
        (bending_hbm, beam_v.at[0]),
        (mass_hbm, beam_v.at[1]),
        (hardening_hbm, beam_v.at[2]),
        (disp_hbm, beam_v.at[3]),
        (vel_hbm, beam_v.at[4]),
    ]
    reads = [pltpu.make_async_copy(a, b, local_sem.at[i]) for i, (a, b) in enumerate(inputs)]
    for read in reads:
        read.start()

    def turned(index, by, count):
        return (index + (by + count)) % count

    span_at = {by: turned(span, by, n_span) for by in (-1, 1)}
    wrap_at = [turned(wrap, by, n_wrap) for by in range(n_wrap)]
    norm_at = {by: turned(normal, by, n_norm) for by in (-1, 1)}
    row_at = [turned(row, by, rows) for by in range(rows)]
    col_at = [turned(col, by, cols) for by in range(cols)]
    sides = [
        (span_at[-1], wrap, normal),
        (span_at[1], wrap, normal),
        (span, wrap_at[n_wrap - 1], normal),
        (span, wrap_at[1], normal),
        (span, wrap, norm_at[-1]),
        (span, wrap, norm_at[1]),
    ]
    barrier = pltpu.get_barrier_semaphore()

    def greet(target):
        pl.semaphore_signal(barrier, inc=1, device_id=target, device_id_type=MESH)

    for side in sides:
        greet(side)
    for a in range(rows):
        for b in range(n_wrap):
            source = (row_at[-a % rows] * cols + col, wrap_at[-b % n_wrap], 0)
            if a == 0 and b == 0:

                @pl.when(normal != 0)
                def _():
                    greet(source)

            else:
                greet(source)
    for k in range(1, cols):
        greet((row * cols + col_at[-k % cols], wrap, normal))

    for d in range(3):
        for u in range(VARS):
            for v in range(VARS):
                scaled = jac_smem[u, d, v] * (-1.0 / 12.0)
                jac[25 * d + 5 * u + v] = jnp.full((8, LANES), scaled, jnp.float32)

    def copy(src, dst, slot, target):
        return pltpu.make_async_remote_copy(
            src_ref=src,
            dst_ref=dst,
            send_sem=send_sem.at[slot],
            recv_sem=recv_sem.at[slot],
            device_id=target,
            device_id_type=MESH,
        )

    def stage_copies(stage, field):
        cells = pl.ds(TOP, WRAP)
        base = 6 * stage
        pairs = [
            (field.at[:, 2:4, cells, :], field.at[:, 2 + SPAN : 4 + SPAN, cells, :]),
            (field.at[:, SPAN : 2 + SPAN, cells, :], field.at[:, 0:2, cells, :]),
            (wall_send.at[stage, 0], wall_recv.at[stage, 0]),
            (wall_send.at[stage, 1], wall_recv.at[stage, 1]),
            (edges.at[stage, 0], edges.at[stage, 2]),
            (edges.at[stage, 0], edges.at[stage, 1]),
        ]
        return [copy(src, dst, base + i, sides[i]) for i, (src, dst) in enumerate(pairs)]

    def stage_wrap_rows(stage, field):
        for v in range(VARS):
            for r in range(2):
                wall_send[stage, 0, v, r] = field[v, 2 : 2 + SPAN, TOP + r, :]
                wall_send[stage, 1, v, r] = field[v, 2 : 2 + SPAN, TOP + WRAP - 2 + r, :]

    def stage_arrive(stage, field):
        zeros = jnp.zeros((VARS, 2, WRAP, LANES), jnp.float32)

        @pl.when(span == 0)
        def _():
            field[:, 0:2, TOP : TOP + WRAP, :] = zeros

        @pl.when(span == n_span - 1)
        def _():
            field[:, 2 + SPAN : 4 + SPAN, TOP : TOP + WRAP, :] = zeros

        for v in range(VARS):
            for r in range(2):
                field[v, 2 : 2 + SPAN, TOP + WRAP + r, :] = wall_recv[stage, 0, v, r]
                field[v, 2 : 2 + SPAN, TOP - 2 + r, :] = wall_recv[stage, 1, v, r]
        edge_terms(
            normal, n_norm, edges.at[stage, 0], edges.at[stage, 1], edges.at[stage, 2], jac, corr
        )

    empty = tuple(jnp.zeros((8, LANES), jnp.float32) for _ in range(VARS))

    reads[0].wait()
    stage_wrap_rows(0, field1)

    def pack_first(s, packed):
        cells = [
            field1[v, s + 2, TOP : TOP + WRAP, :].reshape(2, 8, LANES) for v in range(VARS)
        ]
        return pack_plane(packed, cells, s)

    packed = lax.fori_loop(0, SPAN, pack_first, empty, unroll=True)
    for v in range(VARS):
        edges[0, 0, v] = packed[v]

    at_wall = (n_norm - normal) // n_norm
    pl.semaphore_wait(barrier, 5 + cols + at_wall * (rows * n_wrap * n_norm - 1))

    first = stage_copies(0, field1)
    for one in first:
        one.start()

    for read in reads[1:]:
        read.wait()
    lane = lane_of((8, LANES))
    held = jnp.where(lane < LANES // 2, 2 * lane, 2 * lane - (LANES - 1))
    for j in range(WRAP):
        weight = jnp.broadcast_to(area[:, j : j + 1], (8, LANES))
        where = jnp.broadcast_to(stations[:, j : j + 1], (8, LANES))
        faces[j] = jnp.where(where == held, weight, 0.0)

    for one in first:
        one.wait_recv()
    stage_arrive(0, field1)

    def first_plane(s, packed):
        cells, rates = plane_rates(field1, s, jac, corr)
        scale = DT_FLOW * volume[s].reshape(2, 8, LANES)
        mids = [cells[u] + scale * rates[u] for u in range(VARS)]
        for u in range(VARS):
            field2[u, s + 2, TOP : TOP + WRAP, :] = mids[u].reshape(WRAP, LANES)
        return pack_plane(packed, mids, s)

    packed = lax.fori_loop(0, SPAN, first_plane, empty)
    for v in range(VARS):
        edges[1, 0, v] = packed[v]

    stage_wrap_rows(1, field2)
    second = stage_copies(1, field2)
    for one in second:
        one.start()
    for one in second:
        one.wait_recv()
    stage_arrive(1, field2)

    def second_plane(s, carry):
        cells, rates = plane_rates(field2, s, jac, corr)
        scale = DT_FLOW * volume[s].reshape(2, 8, LANES)
        for u in range(VARS):
            start = field1[u, s + 2, TOP : TOP + WRAP, :].reshape(2, 8, LANES)
            after = 0.5 * (start + cells[u] + scale * rates[u])
            result[u, s] = after.reshape(WRAP, LANES)
        return carry

    lax.fori_loop(0, SPAN, second_plane, 0)

    def group_copy(buffer, slot, which, target):
        return pltpu.make_async_remote_copy(
            src_ref=buffer.at[0],
            dst_ref=buffer.at[slot],
            send_sem=group_sem.at[2 * which],
            recv_sem=group_sem.at[2 * which + 1],
            device_id=target,
            device_id_type=MESH,
        )

    def take(ref, which):
        pltpu.make_async_copy(ref, ref, group_sem.at[which]).wait()

    count_a = rows * n_wrap

    @pl.when(normal == 0)
    def _():
        partial = jnp.zeros((8, LANES), jnp.float32)
        for j in range(WRAP):
            beside = result[0, :, j, :]
            partial = partial + faces[j] * jnp.broadcast_to(beside[:, 0:1], (8, LANES))
        loads_a[0] = partial
        for a in range(rows):
            for b in range(n_wrap):
                for c in range(n_norm):
                    if a or b or c:
                        target = (row_at[a] * cols + col, wrap_at[b], c)
                        group_copy(loads_a, a * n_wrap + b, 0, target).start()

    write = pltpu.make_async_copy(result, out_hbm, local_sem.at[len(inputs)])
    write.start()

    def permuted(x):
        full = jnp.broadcast_to(x, (8, LANES))
        return jnp.take_along_axis(full, held, axis=1)[0:1]

    bending, mass, hardening, disp, vel = [permuted(beam_v[i]) for i in range(5)]
    contact = permuted(contact_v[...])
    inertia = 2.0 * mass / (DT_BEAM * DT_BEAM)
    pull = CONTACT_STIFF * STOP_GAP
    push = jnp.where(contact == 1, pull, jnp.where(contact == 2, -pull, 0.0))
    steady = inertia * (disp + DT_BEAM * vel) + push
    base = inertia + jnp.where(contact > 0, CONTACT_STIFF, 0.0)
    be, bo = halves(bending)
    he, ho = halves(hardening)
    ge, go = halves(base)
    ue, uo = halves(disp)
    fe, fo = halves(steady)
    factors = factor(be, bo, ge + 3.0 * he * ue * ue, go + 3.0 * ho * uo * uo)

    @pl.when(normal == 0)
    def _():
        take(loads_a.at[1:], 1)

    @pl.when(normal != 0)
    def _():
        take(loads_a, 1)

    total = None
    for y in range(count_a):
        a = (row + (rows - y // n_wrap)) % rows
        b = (wrap + (n_wrap - y % n_wrap)) % n_wrap
        term = loads_a[a * n_wrap + b]
        total = term if total is None else total + term
    loads_b[0] = total
    for k in range(1, cols):
        group_copy(loads_b, k, 1, (row * cols + col_at[k], wrap, normal)).start()
    take(loads_b.at[1:], 3)
    total = None
    for z in range(cols):
        term = loads_b[(col + (cols - z)) % cols]
        total = term if total is None else total + term
    loads = jnp.sum(total, axis=0, keepdims=True)

    le, lo = halves(loads)
    fe, fo = fe + le, fo + lo
    ue, uo = substitute(factors, *right_side(fe, fo, he, ho, ue, uo))
    for i, x in enumerate((be, bo, ge, go, he, ho, fe, fo, ue, uo)):
        state_ref[i : i + 1, :] = x

    for one in first + second:
        one.wait_send()

    @pl.when(normal == 0)
    def _():
        take(tally, 0)

    take(loads_b.at[1:], 2)
    write.wait()


def beam_kernel(state_ref, flow_hbm, out_hbm, defl_ref, sem):
    write = pltpu.make_async_copy(flow_hbm, out_hbm, sem)
    write.start()
    be, bo, ge, go, he, ho, fe, fo, ue, uo = [state_ref[i : i + 1, :] for i in range(10)]
    for _ in range(NEWTON - 1):
        factors = factor(be, bo, ge + 3.0 * he * ue * ue, go + 3.0 * ho * uo * uo)
        ue, uo = substitute(factors, *right_side(fe, fo, he, ho, ue, uo))
    both = jnp.where(lane_of((1, LANES)) < LANES // 2, ue, roll(uo, LANES // 2))
    lane = lane_of((8, LANES))
    back = (lane % 2) * (LANES // 2) + lane // 2
    full = jnp.broadcast_to(both, (8, LANES))
    defl_ref[...] = jnp.take_along_axis(full, back, axis=1)[0:1]
    write.wait()


def solution(mesh):
    n_span, n_wrap, n_norm = (mesh.shape[axis] for axis in ("span", "wrap", "normal"))
    cols, ys = n_span // 2, 2 * n_wrap
    f32 = jnp.float32

    def step(
        flow_state,
        inv_volume,
        flux_jacobians,
        area,
        station_map,
        contact,
        bending,
        mass,
        hardening,
        disp_old,
        vel_old,
    ):
        vectors = [
            x.reshape(1, STATIONS) for x in (contact, bending, mass, hardening, disp_old, vel_old)
        ]
        hbm = pl.BlockSpec(memory_space=pltpu.HBM)
        flow_next, state = pl.pallas_call(
            functools.partial(kernel, n_span, n_wrap, n_norm),
            out_shape=(
                jax.ShapeDtypeStruct(flow_state.shape, f32),
                jax.ShapeDtypeStruct((16, LANES), f32),
            ),
            in_specs=[hbm, hbm, pl.BlockSpec(memory_space=pltpu.SMEM)] + [hbm] * 8,
            out_specs=(hbm, pl.BlockSpec(memory_space=pltpu.VMEM)),
            scratch_shapes=[
                pltpu.VMEM((VARS, SPAN + 4, WRAP + 16, LANES), f32),
                pltpu.VMEM((VARS, SPAN + 4, WRAP + 16, LANES), f32),
                pltpu.VMEM((SPAN, WRAP, LANES), f32),
                pltpu.VMEM((2, 2, VARS, 2, SPAN, LANES), f32),
                pltpu.VMEM((2, 2, VARS, 2, SPAN, LANES), f32),
                pltpu.VMEM((2, 3, VARS, 8, LANES), f32),
                pltpu.VMEM((VARS, 8, LANES), f32),
                pltpu.VMEM((75, 8, LANES), f32),
                pltpu.VMEM((VARS, SPAN, WRAP, LANES), f32),
                pltpu.VMEM((WRAP, 8, LANES), f32),
                pltpu.VMEM((SPAN, WRAP), f32),
                pltpu.VMEM((SPAN, WRAP), jnp.int32),
                pltpu.VMEM((1, STATIONS), jnp.int32),
                pltpu.VMEM((5, 1, STATIONS), f32),
                pltpu.VMEM((ys, 8, LANES), f32),
                pltpu.VMEM((cols, 8, LANES), f32),
                pltpu.VMEM((ys * n_norm - 1, 8, LANES), f32),
                pltpu.SemaphoreType.DMA((11,)),
                pltpu.SemaphoreType.DMA((12,)),
                pltpu.SemaphoreType.DMA((12,)),
                pltpu.SemaphoreType.DMA((4,)),
            ],
            compiler_params=pltpu.CompilerParams(
                collective_id=0, has_side_effects=True, vmem_limit_bytes=60 * 1024 * 1024
            ),
            cost_estimate=pl.CostEstimate(
                flops=10_000_000, bytes_accessed=1_000_000, transcendentals=0
            ),
        )(flow_state, inv_volume, flux_jacobians.transpose(1, 0, 2), area, station_map, *vectors)
        flow_next, deflection = pl.pallas_call(
            beam_kernel,
            out_shape=(
                jax.ShapeDtypeStruct(flow_state.shape, f32),
                jax.ShapeDtypeStruct((1, STATIONS), f32),
            ),
            in_specs=[pl.BlockSpec(memory_space=pltpu.VMEM), hbm],
            out_specs=(hbm, pl.BlockSpec(memory_space=pltpu.VMEM)),
            scratch_shapes=[pltpu.SemaphoreType.DMA(())],
            compiler_params=pltpu.CompilerParams(vmem_limit_bytes=60 * 1024 * 1024),
        )(state, flow_next)
        return flow_next, deflection.reshape(STATIONS)

    placed = (
        P(None, "span", "wrap", "normal"),
        P("span", "wrap", "normal"),
        P(),
        P("span", "wrap"),
        P("span", "wrap"),
    ) + (P(),) * 6
    return jax.shard_map(
        step,
        mesh=mesh,
        in_specs=placed,
        out_specs=(P(None, "span", "wrap", "normal"), P()),
        check_vma=False,
    )
```

profile of v0, /device:TPU:1, one launch (start us, length us, event | category | flops | bytes accessed | tf_op | source)
XLA Modules:
  0.0 54.4 jit_solution(15922934172005307506)
XLA Ops:
  0.6 41.6 %shard_map.122 = (f32[5,8,16,128]{3,2,1,0:T(8,128)}, f32[16,128]{1,0:T(8,128)}) custom-call(f32[5,8,16,128]{3,2,1,0:T(8,128)} %flow_hbm.1, f32[8,16,128]{2,1,0:T(8,128)} %volume_hbm.1, f32[5,3,5]{2,1,0:T(4,128)} %bitcast.8, f32[8,16]{1,0:T(8,128)} %area_hbm.1, s32[8,16]{1,0:T(8,128)} %map_hbm.1, s32[1,128]{1,0:T(1,128)} %bitcast.9, f32[1,128]{1,0:T(1,128)} %bitcast.10, ...), custom_call_target="tpu_custom_call" | custom-call | flops 10000000 | bytes 1000000 | tf_op jit(solution)/shard_map/pallas_call | solution.py:503
  42.2 12.2 %shard_map.123 = (f32[5,8,16,128]{3,2,1,0:T(8,128)}, f32[1,128]{1,0:T(1,128)}) custom-call(f32[16,128]{1,0:T(8,128)} %get-tuple-element.6.state_ref, f32[5,8,16,128]{3,2,1,0:T(8,128)} %get-tuple-element.7.flow_hbm), custom_call_target="tpu_custom_call" | custom-call | tf_op jit(solution)/shard_map/pallas_call | solution.py:541
where the time goes:
time: 54.7 us; the launch traced here: 54.4 us
  Pallas kernels  53.8 us (98%)
  between operations  0.64 us (1%)
    pallas_call x1, Pallas kernels, step(): pl.pallas_call(functools.partial(kernel, n_span, n_wrap, n_norm), out_sha...  41.6 us
    pallas_call x1, Pallas kernels, step(): pl.pallas_call(beam_kernel, out_shape=(jax.ShapeDtypeStruct(flow_state.sh...  12.2 us

commit v1 on v0

--- a/solution.py
+++ b/solution.py
@@ -155,6 +155,83 @@
     return cells, rates
 
 
+def pack_wall(field, volume, packed):
+    group = lane_of((8, LANES)) // 8
+    for v in range(VARS + 1):
+        for t in range(2):
+            have = jnp.zeros((8, LANES), jnp.float32)
+            for s in range(SPAN):
+                if v < VARS:
+                    tile = field[v, s + 2, TOP + 8 * t : TOP + 8 * t + 8, :]
+                else:
+                    tile = volume[s, 8 * t : 8 * t + 8, :]
+                have = jnp.where(group == s + 4, roll(tile, 8 * (s + 4) + 2), have)
+            packed[v, 8 * t : 8 * t + 8, :] = have
+
+
+def mirrored(x):
+    place = lane_of(x.shape) % 8
+    return jnp.where(place == 0, roll(x, -3), jnp.where(place == 1, roll(x, -1), x))
+
+
+def wall_rates(layer, top, rows, wanted, jac):
+    cells, grads, smooths = [], [[], [], []], []
+    shape = (rows // 8, 8, LANES)
+    for v in range(VARS):
+        c = layer[v, top : top + rows, :]
+        reads = [
+            [roll(c, -8 * k) for k in (-2, -1, 1, 2)],
+            [layer[v, top + k : top + k + rows, :] for k in (-2, -1, 1, 2)],
+            [roll(c, -k) for k in (-2, -1, 1, 2)],
+        ]
+        near, far = None, None
+        for d, (m2, m1, p1, p2) in enumerate(reads):
+            grads[d].append(((m2 - p2) + 8.0 * (p1 - m1)).reshape(shape))
+            near = (m1 + p1) if near is None else near + (m1 + p1)
+            far = (m2 + p2) if far is None else far + (m2 + p2)
+        smooths.append((-DISSIPATION * (far - 4.0 * near + 18.0 * c)).reshape(shape))
+        cells.append(c)
+    rates = []
+    for u in range(wanted):
+        total = smooths[u]
+        for d in range(3):
+            for v in range(VARS):
+                total = total + jac[25 * d + 5 * u + v][None] * grads[d][v]
+        rates.append(total.reshape(rows, LANES))
+    return cells, rates
+
+
+def wall_loads(span, n_span, packed, beside, corner, layer, mid, faces, jac):
+    group = lane_of((8, LANES)) // 8
+    first, last = span == 0, span == n_span - 1
+    for v in range(VARS + 1):
+        tiles = [
+            (corner[0, v], beside[2, v, 0:8], corner[1, v]),
+            (beside[0, v, 0:8], packed[v, 0:8], beside[1, v, 0:8]),
+            (beside[0, v, 8:16], packed[v, 8:16], beside[1, v, 8:16]),
+            (corner[2, v], beside[3, v, 0:8], corner[3, v]),
+        ]
+        for t, (left, centre, right) in enumerate(tiles):
+            left = jnp.where(first, 0.0, roll(left, LANES // 2))
+            right = jnp.where(last, 0.0, roll(right, LANES // 2))
+            whole = jnp.where(group < 4, left, jnp.where(group >= 12, right, centre))
+            layer[v, 8 * t : 8 * t + 8, :] = mirrored(whole)
+    span_group = lane_of((24, LANES)) // 8
+    outside = (first & (span_group < 4)) | (last & (span_group >= 12))
+    cells, rates = wall_rates(layer, 4, 24, VARS, jac)
+    scale = DT_FLOW * layer[VARS, 4:28, :]
+    for u in range(VARS):
+        mid[u] = mirrored(jnp.where(outside, 0.0, cells[u] + scale * rates[u]))
+    cells, rates = wall_rates(mid, 4, 16, 1, jac)
+    scale = DT_FLOW * layer[VARS, 8:24, :]
+    after = 0.5 * (layer[0, 8:24, :] + cells[0] + scale * rates[0])
+    total = jnp.zeros((WRAP, LANES), jnp.float32)
+    for s in range(SPAN):
+        at = 8 * (s + 4) + 2
+        total = total + faces[s] * jnp.broadcast_to(after[:, at : at + 1], (WRAP, LANES))
+    return total[0:8] + total[8:16]
+
+
 def kernel(
     n_span,
     n_wrap,
@@ -189,10 +266,17 @@
     loads_a,
     loads_b,
     tally,
+    wall_packed,
+    wall_beside,
+    wall_corner,
+    wall_layer,
+    wall_mid,
     local_sem,
     send_sem,
     recv_sem,
     group_sem,
+    wide_send_sem,
+    wide_recv_sem,
 ):
     span, wrap, normal = lax.axis_index("span"), lax.axis_index("wrap"), lax.axis_index("normal")
     rows = 2
@@ -236,8 +320,16 @@
     def greet(target):
         pl.semaphore_signal(barrier, inc=1, device_id=target, device_id_type=MESH)
 
+    corners = [(span_at[i], wrap_at[j], normal) for j in (n_wrap - 1, 1) for i in (-1, 1)]
+
     for side in sides:
         greet(side)
+
+    @pl.when(normal == 0)
+    def _():
+        for one in corners:
+            greet(one)
+
     for a in range(rows):
         for b in range(n_wrap):
             source = (row_at[-a % rows] * cols + col, wrap_at[-b % n_wrap], 0)
@@ -306,9 +398,40 @@
             normal, n_norm, edges.at[stage, 0], edges.at[stage, 1], edges.at[stage, 2], jac, corr
         )
 
+    whole, low, high = pl.ds(0, WRAP), pl.ds(0, 8), pl.ds(8, 8)
+    wide = []
+    for i, (target, part, land) in enumerate(
+        [
+            (sides[0], whole, wall_beside.at[1]),
+            (sides[1], whole, wall_beside.at[0]),
+            (sides[2], low, wall_beside.at[3, :, low]),
+            (sides[3], high, wall_beside.at[2, :, low]),
+            (corners[0], low, wall_corner.at[3]),
+            (corners[1], low, wall_corner.at[2]),
+            (corners[2], high, wall_corner.at[1]),
+            (corners[3], high, wall_corner.at[0]),
+        ]
+    ):
+        wide.append(
+            pltpu.make_async_remote_copy(
+                src_ref=wall_packed.at[:, part],
+                dst_ref=land,
+                send_sem=wide_send_sem.at[i],
+                recv_sem=wide_recv_sem.at[i],
+                device_id=target,
+                device_id_type=MESH,
+            )
+        )
+
     empty = tuple(jnp.zeros((8, LANES), jnp.float32) for _ in range(VARS))
 
     reads[0].wait()
+    reads[1].wait()
+
+    @pl.when(normal == 0)
+    def _():
+        pack_wall(field1, volume, wall_packed)
+
     stage_wrap_rows(0, field1)
 
     def pack_first(s, packed):
@@ -322,55 +445,21 @@
         edges[0, 0, v] = packed[v]
 
     at_wall = (n_norm - normal) // n_norm
-    pl.semaphore_wait(barrier, 5 + cols + at_wall * (rows * n_wrap * n_norm - 1))
+    pl.semaphore_wait(barrier, 5 + cols + at_wall * (rows * n_wrap * n_norm + 3))
+
+    @pl.when(normal == 0)
+    def _():
+        for one in wide:
+            one.start()
 
     first = stage_copies(0, field1)
     for one in first:
         one.start()
 
-    for read in reads[1:]:
+    for read in reads[2:]:
         read.wait()
     lane = lane_of((8, LANES))
     held = jnp.where(lane < LANES // 2, 2 * lane, 2 * lane - (LANES - 1))
-    for j in range(WRAP):
-        weight = jnp.broadcast_to(area[:, j : j + 1], (8, LANES))
-        where = jnp.broadcast_to(stations[:, j : j + 1], (8, LANES))
-        faces[j] = jnp.where(where == held, weight, 0.0)
-
-    for one in first:
-        one.wait_recv()
-    stage_arrive(0, field1)
-
-    def first_plane(s, packed):
-        cells, rates = plane_rates(field1, s, jac, corr)
-        scale = DT_FLOW * volume[s].reshape(2, 8, LANES)
-        mids = [cells[u] + scale * rates[u] for u in range(VARS)]
-        for u in range(VARS):
-            field2[u, s + 2, TOP : TOP + WRAP, :] = mids[u].reshape(WRAP, LANES)
-        return pack_plane(packed, mids, s)
-
-    packed = lax.fori_loop(0, SPAN, first_plane, empty)
-    for v in range(VARS):
-        edges[1, 0, v] = packed[v]
-
-    stage_wrap_rows(1, field2)
-    second = stage_copies(1, field2)
-    for one in second:
-        one.start()
-    for one in second:
-        one.wait_recv()
-    stage_arrive(1, field2)
-
-    def second_plane(s, carry):
-        cells, rates = plane_rates(field2, s, jac, corr)
-        scale = DT_FLOW * volume[s].reshape(2, 8, LANES)
-        for u in range(VARS):
-            start = field1[u, s + 2, TOP : TOP + WRAP, :].reshape(2, 8, LANES)
-            after = 0.5 * (start + cells[u] + scale * rates[u])
-            result[u, s] = after.reshape(WRAP, LANES)
-        return carry
-
-    lax.fori_loop(0, SPAN, second_plane, 0)
 
     def group_copy(buffer, slot, which, target):
         return pltpu.make_async_remote_copy(
@@ -384,25 +473,6 @@
 
     def take(ref, which):
         pltpu.make_async_copy(ref, ref, group_sem.at[which]).wait()
-
-    count_a = rows * n_wrap
-
-    @pl.when(normal == 0)
-    def _():
-        partial = jnp.zeros((8, LANES), jnp.float32)
-        for j in range(WRAP):
-            beside = result[0, :, j, :]
-            partial = partial + faces[j] * jnp.broadcast_to(beside[:, 0:1], (8, LANES))
-        loads_a[0] = partial
-        for a in range(rows):
-            for b in range(n_wrap):
-                for c in range(n_norm):
-                    if a or b or c:
-                        target = (row_at[a] * cols + col, wrap_at[b], c)
-                        group_copy(loads_a, a * n_wrap + b, 0, target).start()
-
-    write = pltpu.make_async_copy(result, out_hbm, local_sem.at[len(inputs)])
-    write.start()
 
     def permuted(x):
         full = jnp.broadcast_to(x, (8, LANES))
@@ -424,12 +494,70 @@
 
     @pl.when(normal == 0)
     def _():
+        row_id = lax.broadcasted_iota(jnp.int32, (WRAP, WRAP), 0)
+        same = (row_id == lane_of((WRAP, WRAP))).astype(jnp.float32)
+
+        def turned_over(x):
+            return lax.dot_general(
+                same, x, (((1,), (1,)), ((), ())), precision=lax.Precision.HIGHEST
+            )
+
+        weights = turned_over(area[...])
+        places = turned_over(stations[...].astype(jnp.float32))
+        aims = jnp.broadcast_to(held[0:1], (WRAP, LANES)).astype(jnp.float32)
+        for s in range(SPAN):
+            weight = jnp.broadcast_to(weights[:, s : s + 1], (WRAP, LANES))
+            place = jnp.broadcast_to(places[:, s : s + 1], (WRAP, LANES))
+            faces[s] = jnp.where(place == aims, weight, 0.0)
+        for one in wide:
+            one.wait_recv()
+        loads_a[0] = wall_loads(
+            span,
+            n_span,
+            wall_packed,
+            wall_beside,
+            wall_corner,
+            wall_layer,
+            wall_mid,
+            faces,
+            jac,
+        )
+        for a in range(rows):
+            for b in range(n_wrap):
+                for c in range(n_norm):
+                    if a or b or c:
+                        target = (row_at[a] * cols + col, wrap_at[b], c)
+                        group_copy(loads_a, a * n_wrap + b, 0, target).start()
+
+    for one in first:
+        one.wait_recv()
+    stage_arrive(0, field1)
+
+    def first_plane(s, packed):
+        cells, rates = plane_rates(field1, s, jac, corr)
+        scale = DT_FLOW * volume[s].reshape(2, 8, LANES)
+        mids = [cells[u] + scale * rates[u] for u in range(VARS)]
+        for u in range(VARS):
+            field2[u, s + 2, TOP : TOP + WRAP, :] = mids[u].reshape(WRAP, LANES)
+        return pack_plane(packed, mids, s)
+
+    packed = lax.fori_loop(0, SPAN, first_plane, empty)
+    for v in range(VARS):
+        edges[1, 0, v] = packed[v]
+
+    stage_wrap_rows(1, field2)
+    second = stage_copies(1, field2)
+    for one in second:
+        one.start()
+    @pl.when(normal == 0)
+    def _():
         take(loads_a.at[1:], 1)
 
     @pl.when(normal != 0)
     def _():
         take(loads_a, 1)
 
+    count_a = rows * n_wrap
     total = None
     for y in range(count_a):
         a = (row + (rows - y // n_wrap)) % rows
@@ -439,6 +567,24 @@
     loads_b[0] = total
     for k in range(1, cols):
         group_copy(loads_b, k, 1, (row * cols + col_at[k], wrap, normal)).start()
+    for one in second:
+        one.wait_recv()
+    stage_arrive(1, field2)
+
+    def second_plane(s, carry):
+        cells, rates = plane_rates(field2, s, jac, corr)
+        scale = DT_FLOW * volume[s].reshape(2, 8, LANES)
+        for u in range(VARS):
+            start = field1[u, s + 2, TOP : TOP + WRAP, :].reshape(2, 8, LANES)
+            after = 0.5 * (start + cells[u] + scale * rates[u])
+            result[u, s] = after.reshape(WRAP, LANES)
+        return carry
+
+    lax.fori_loop(0, SPAN, second_plane, 0)
+
+    write = pltpu.make_async_copy(result, out_hbm, local_sem.at[len(inputs)])
+    write.start()
+
     take(loads_b.at[1:], 3)
     total = None
     for z in range(cols):
@@ -457,15 +603,24 @@
 
     @pl.when(normal == 0)
     def _():
+        for one in wide:
+            one.wait_send()
         take(tally, 0)
 
     take(loads_b.at[1:], 2)
     write.wait()
 
 
-def beam_kernel(state_ref, flow_hbm, out_hbm, defl_ref, sem):
-    write = pltpu.make_async_copy(flow_hbm, out_hbm, sem)
-    write.start()
+def beam_kernel(state_ref, flow_hbm, out_hbm, defl_ref, held, read_sem, write_sem):
+    def each(src, dst, sem):
+        return [pltpu.make_async_copy(src.at[v], dst.at[v], sem.at[v]) for v in range(VARS)]
+
+    reads, writes = each(flow_hbm, held, read_sem), each(held, out_hbm, write_sem)
+    for read in reads:
+        read.start()
+    for read, write in zip(reads, writes):
+        read.wait()
+        write.start()
     be, bo, ge, go, he, ho, fe, fo, ue, uo = [state_ref[i : i + 1, :] for i in range(10)]
     for _ in range(NEWTON - 1):
         factors = factor(be, bo, ge + 3.0 * he * ue * ue, go + 3.0 * ho * uo * uo)
@@ -475,7 +630,8 @@
     back = (lane % 2) * (LANES // 2) + lane // 2
     full = jnp.broadcast_to(both, (8, LANES))
     defl_ref[...] = jnp.take_along_axis(full, back, axis=1)[0:1]
-    write.wait()
+    for write in writes:
+        write.wait()
 
 
 def solution(mesh):
@@ -518,7 +674,7 @@
                 pltpu.VMEM((VARS, 8, LANES), f32),
                 pltpu.VMEM((75, 8, LANES), f32),
                 pltpu.VMEM((VARS, SPAN, WRAP, LANES), f32),
-                pltpu.VMEM((WRAP, 8, LANES), f32),
+                pltpu.VMEM((SPAN, WRAP, LANES), f32),
                 pltpu.VMEM((SPAN, WRAP), f32),
                 pltpu.VMEM((SPAN, WRAP), jnp.int32),
                 pltpu.VMEM((1, STATIONS), jnp.int32),
@@ -526,10 +682,17 @@
                 pltpu.VMEM((ys, 8, LANES), f32),
                 pltpu.VMEM((cols, 8, LANES), f32),
                 pltpu.VMEM((ys * n_norm - 1, 8, LANES), f32),
+                pltpu.VMEM((VARS + 1, WRAP, LANES), f32),
+                pltpu.VMEM((4, VARS + 1, WRAP, LANES), f32),
+                pltpu.VMEM((4, VARS + 1, 8, LANES), f32),
+                pltpu.VMEM((VARS + 1, WRAP + 16, LANES), f32),
+                pltpu.VMEM((VARS, 24, LANES), f32),
                 pltpu.SemaphoreType.DMA((11,)),
                 pltpu.SemaphoreType.DMA((12,)),
                 pltpu.SemaphoreType.DMA((12,)),
                 pltpu.SemaphoreType.DMA((4,)),
+                pltpu.SemaphoreType.DMA((8,)),
+                pltpu.SemaphoreType.DMA((8,)),
             ],
             compiler_params=pltpu.CompilerParams(
                 collective_id=0, has_side_effects=True, vmem_limit_bytes=60 * 1024 * 1024
@@ -546,7 +709,11 @@
             ),
             in_specs=[pl.BlockSpec(memory_space=pltpu.VMEM), hbm],
             out_specs=(hbm, pl.BlockSpec(memory_space=pltpu.VMEM)),
-            scratch_shapes=[pltpu.SemaphoreType.DMA(())],
+            scratch_shapes=[
+                pltpu.VMEM((VARS, SPAN, WRAP, LANES), f32),
+                pltpu.SemaphoreType.DMA((VARS,)),
+                pltpu.SemaphoreType.DMA((VARS,)),
+            ],
             compiler_params=pltpu.CompilerParams(vmem_limit_bytes=60 * 1024 * 1024),
         )(state, flow_next)
         return flow_next, deflection.reshape(STATIONS)

time: 54.7 us -> 40.6 us (0.74)
  Pallas kernels: 53.8 us -> 39.6 us
    pallas_call x1, Pallas kernels: 12.2 us -> 3.65 us  [step(): pl.pallas_call(beam_kernel, out_shape=(jax.ShapeDtypeStruct(flow_state.sh...]
    pallas_call x1, Pallas kernels: 41.6 us -> 36 us  [step(): pl.pallas_call(functools.partial(kernel, n_span, n_wrap, n_norm), out_sha...]
where the time goes in v1:
time: 40.6 us; the launch traced here: 40.3 us
  Pallas kernels  39.6 us (98%)
  between operations  0.64 us (2%)
    pallas_call x1, Pallas kernels, step(): pl.pallas_call(functools.partial(kernel, n_span, n_wrap, n_norm), out_sha...  36 us
    pallas_call x1, Pallas kernels, step(): pl.pallas_call(beam_kernel, out_shape=(jax.ShapeDtypeStruct(flow_state.sh...  3.65 us

profile of v1, /device:TPU:1, one launch (start us, length us, event | category | flops | bytes accessed | tf_op | source)
XLA Modules:
  0.0 40.3 jit_solution(13639296122137598280)
XLA Ops:
  0.6 36.0 %shard_map.122 = (f32[5,8,16,128]{3,2,1,0:T(8,128)}, f32[16,128]{1,0:T(8,128)}) custom-call(f32[5,8,16,128]{3,2,1,0:T(8,128)} %flow_hbm.1, f32[8,16,128]{2,1,0:T(8,128)} %volume_hbm.1, f32[5,3,5]{2,1,0:T(4,128)} %bitcast.8, f32[8,16]{1,0:T(8,128)} %area_hbm.1, s32[8,16]{1,0:T(8,128)} %map_hbm.1, s32[1,128]{1,0:T(1,128)} %bitcast.9, f32[1,128]{1,0:T(1,128)} %bitcast.10, ...), custom_call_target="tpu_custom_call" | custom-call | flops 10000000 | bytes 1000000 | tf_op jit(solution)/shard_map/pallas_call | solution.py:659
  36.6 3.6 %shard_map.123 = (f32[5,8,16,128]{3,2,1,0:T(8,128)}, f32[1,128]{1,0:T(1,128)}) custom-call(f32[16,128]{1,0:T(8,128)} %get-tuple-element.6.state_ref, f32[5,8,16,128]{3,2,1,0:T(8,128)} %get-tuple-element.7.flow_hbm), custom_call_target="tpu_custom_call" | custom-call | tf_op jit(solution)/shard_map/pallas_call | solution.py:704

commit v2 on v1

--- a/solution.py
+++ b/solution.py
@@ -169,6 +169,30 @@
             packed[v, 8 * t : 8 * t + 8, :] = have
 
 
+def pair_wall(packed, pairs, edge, tip):
+    lane, row = lane_of((8, LANES)), lax.broadcasted_iota(jnp.int32, (8, LANES), 0)
+    own = (lane >= LANES // 4) & (lane < 3 * LANES // 4)
+    for p in range(3):
+        for t in range(2):
+            rows = slice(8 * t, 8 * t + 8)
+            pairs[p, rows, :] = jnp.where(own, packed[p, rows, :], roll(packed[p + 3, rows, :], 64))
+    for t in range(2):
+        a, b, c = (pairs[p, 8 * t : 8 * t + 8, :] for p in range(3))
+        four = row < 4
+        edge[t, 0] = jnp.where(four, a if t == 0 else pltpu.roll(a, 4, 0), b if t else pltpu.roll(b, 4, 0))
+        edge[t, 1] = c
+        at = 6 * t
+        tip[t] = jnp.where(
+            row < 2,
+            turn_rows(a, -at),
+            jnp.where(four, turn_rows(b, 2 - at), turn_rows(c, 4 - at)),
+        )
+
+
+def turn_rows(x, by):
+    return pltpu.roll(x, by % 8, 0) if by % 8 else x
+
+
 def mirrored(x):
     place = lane_of(x.shape) % 8
     return jnp.where(place == 0, roll(x, -3), jnp.where(place == 1, roll(x, -1), x))
@@ -201,19 +225,26 @@
     return cells, rates
 
 
-def wall_loads(span, n_span, packed, beside, corner, layer, mid, faces, jac):
+def wall_loads(span, n_span, packed, beside, edges, tips, layer, mid, faces, jac):
     group = lane_of((8, LANES)) // 8
     first, last = span == 0, span == n_span - 1
+
+    def swing(x, when):
+        return roll(x, LANES // 2) if when else x
+
     for v in range(VARS + 1):
+        p, upper = v % 3, v >= 3
+        low_edge = edges[0, 1] if p == 2 else turn_rows(edges[0, 0], 4 - 4 * p)
+        high_edge = edges[1, 1] if p == 2 else turn_rows(edges[1, 0], 4 * p)
         tiles = [
-            (corner[0, v], beside[2, v, 0:8], corner[1, v]),
-            (beside[0, v, 0:8], packed[v, 0:8], beside[1, v, 0:8]),
-            (beside[0, v, 8:16], packed[v, 8:16], beside[1, v, 8:16]),
-            (corner[2, v], beside[3, v, 0:8], corner[3, v]),
+            (turn_rows(tips[0], 6 - 2 * p), swing(low_edge, upper), turn_rows(tips[1], 6 - 2 * p)),
+            (beside[0, p, 0:8], packed[v, 0:8], beside[1, p, 0:8]),
+            (beside[0, p, 8:16], packed[v, 8:16], beside[1, p, 8:16]),
+            (turn_rows(tips[2], -2 * p), swing(high_edge, upper), turn_rows(tips[3], -2 * p)),
         ]
         for t, (left, centre, right) in enumerate(tiles):
-            left = jnp.where(first, 0.0, roll(left, LANES // 2))
-            right = jnp.where(last, 0.0, roll(right, LANES // 2))
+            left = jnp.where(first, 0.0, swing(left, not upper))
+            right = jnp.where(last, 0.0, swing(right, not upper))
             whole = jnp.where(group < 4, left, jnp.where(group >= 12, right, centre))
             layer[v, 8 * t : 8 * t + 8, :] = mirrored(whole)
     span_group = lane_of((24, LANES)) // 8
@@ -229,7 +260,7 @@
     for s in range(SPAN):
         at = 8 * (s + 4) + 2
         total = total + faces[s] * jnp.broadcast_to(after[:, at : at + 1], (WRAP, LANES))
-    return total[0:8] + total[8:16]
+    return jnp.sum(total, axis=0, keepdims=True)
 
 
 def kernel(
@@ -238,7 +269,7 @@
     n_norm,
     flow_hbm,
     volume_hbm,
-    jac_smem,
+    jac_hbm,
     area_hbm,
     map_hbm,
     contact_hbm,
@@ -247,8 +278,8 @@
     hardening_hbm,
     disp_hbm,
     vel_hbm,
-    out_hbm,
-    state_ref,
+    result,
+    defl_ref,
     field1,
     field2,
     volume,
@@ -257,18 +288,23 @@
     edges,
     corr,
     jac,
-    result,
     faces,
     area,
     stations,
     contact_v,
     beam_v,
+    jac_held,
     loads_a,
     loads_b,
+    loads_c,
     tally,
     wall_packed,
+    wall_pairs,
     wall_beside,
-    wall_corner,
+    edge_put,
+    edge_got,
+    tip_put,
+    tip_got,
     wall_layer,
     wall_mid,
     local_sem,
@@ -281,7 +317,10 @@
     span, wrap, normal = lax.axis_index("span"), lax.axis_index("wrap"), lax.axis_index("normal")
     rows = 2
     cols = n_span // rows
-    row, col = span // cols, span % cols
+    row, col = lax.div(span, cols), lax.rem(span, cols)
+    zs, cores = cols // 2, 2
+    z, core = lax.div(col, cores), lax.rem(col, cores)
+    y_own = row * n_wrap + wrap
 
     inputs = [
         (flow_hbm, field1.at[:, 2 : 2 + SPAN, TOP : TOP + WRAP, :]),
@@ -294,19 +333,21 @@
         (hardening_hbm, beam_v.at[2]),
         (disp_hbm, beam_v.at[3]),
         (vel_hbm, beam_v.at[4]),
+        (jac_hbm, jac_held),
     ]
     reads = [pltpu.make_async_copy(a, b, local_sem.at[i]) for i, (a, b) in enumerate(inputs)]
     for read in reads:
         read.start()
 
     def turned(index, by, count):
-        return (index + (by + count)) % count
+        return lax.rem(index + (by + count), count)
 
     span_at = {by: turned(span, by, n_span) for by in (-1, 1)}
     wrap_at = [turned(wrap, by, n_wrap) for by in range(n_wrap)]
     norm_at = {by: turned(normal, by, n_norm) for by in (-1, 1)}
     row_at = [turned(row, by, rows) for by in range(rows)]
-    col_at = [turned(col, by, cols) for by in range(cols)]
+    z_at = [turned(z, by, zs) for by in range(zs)]
+    core_at = [core, turned(core, 1, cores)]
     sides = [
         (span_at[-1], wrap, normal),
         (span_at[1], wrap, normal),
@@ -325,30 +366,27 @@
     for side in sides:
         greet(side)
 
+    def device(y, z, core, x):
+        return (y[0] * cols + z * cores + core, y[1], x)
+
+    here = (row, wrap)
+    y_at = [(row_at[a], wrap_at[b]) for a in range(rows) for b in range(n_wrap)]
+    beside_y = (1, n_wrap - 1)
+
     @pl.when(normal == 0)
     def _():
         for one in corners:
             greet(one)
-
-    for a in range(rows):
-        for b in range(n_wrap):
-            source = (row_at[-a % rows] * cols + col, wrap_at[-b % n_wrap], 0)
-            if a == 0 and b == 0:
-
-                @pl.when(normal != 0)
-                def _():
-                    greet(source)
-
-            else:
-                greet(source)
-    for k in range(1, cols):
-        greet((row * cols + col_at[-k % cols], wrap, normal))
-
-    for d in range(3):
-        for u in range(VARS):
-            for v in range(VARS):
-                scaled = jac_smem[u, d, v] * (-1.0 / 12.0)
-                jac[25 * d + 5 * u + v] = jnp.full((8, LANES), scaled, jnp.float32)
+        for k in range(1, len(y_at)):
+            if k not in beside_y:
+                greet(device(y_at[k], z, core, 0))
+        for k in range(1, zs):
+            greet(device(here, z_at[k], core, 0))
+
+    @pl.when(normal != 0)
+    def _():
+        for k in range(cores):
+            greet(device(here, z, core_at[k], 0))
 
     def copy(src, dst, slot, target):
         return pltpu.make_async_remote_copy(
@@ -398,24 +436,23 @@
             normal, n_norm, edges.at[stage, 0], edges.at[stage, 1], edges.at[stage, 2], jac, corr
         )
 
-    whole, low, high = pl.ds(0, WRAP), pl.ds(0, 8), pl.ds(8, 8)
     wide = []
-    for i, (target, part, land) in enumerate(
+    for i, (src, dst, target) in enumerate(
         [
-            (sides[0], whole, wall_beside.at[1]),
-            (sides[1], whole, wall_beside.at[0]),
-            (sides[2], low, wall_beside.at[3, :, low]),
-            (sides[3], high, wall_beside.at[2, :, low]),
-            (corners[0], low, wall_corner.at[3]),
-            (corners[1], low, wall_corner.at[2]),
-            (corners[2], high, wall_corner.at[1]),
-            (corners[3], high, wall_corner.at[0]),
+            (tip_put.at[0], tip_got.at[3], corners[0]),
+            (tip_put.at[0], tip_got.at[2], corners[1]),
+            (tip_put.at[1], tip_got.at[1], corners[2]),
+            (tip_put.at[1], tip_got.at[0], corners[3]),
+            (edge_put.at[0], edge_got.at[1], sides[2]),
+            (edge_put.at[1], edge_got.at[0], sides[3]),
+            (wall_pairs, wall_beside.at[1], sides[0]),
+            (wall_pairs, wall_beside.at[0], sides[1]),
         ]
     ):
         wide.append(
             pltpu.make_async_remote_copy(
-                src_ref=wall_packed.at[:, part],
-                dst_ref=land,
+                src_ref=src,
+                dst_ref=dst,
                 send_sem=wide_send_sem.at[i],
                 recv_sem=wide_recv_sem.at[i],
                 device_id=target,
@@ -431,6 +468,16 @@
     @pl.when(normal == 0)
     def _():
         pack_wall(field1, volume, wall_packed)
+        pair_wall(wall_packed, wall_pairs, edge_put, tip_put)
+
+    at_wall = lax.div(n_norm - normal, n_norm)
+    wall_peers = 4 + (len(y_at) - 1 - len(set(beside_y))) + (zs - 1) + cores * (n_norm - 1)
+    pl.semaphore_wait(barrier, 6 + at_wall * wall_peers)
+
+    @pl.when(normal == 0)
+    def _():
+        for one in wide:
+            one.start()
 
     stage_wrap_rows(0, field1)
 
@@ -444,32 +491,35 @@
     for v in range(VARS):
         edges[0, 0, v] = packed[v]
 
-    at_wall = (n_norm - normal) // n_norm
-    pl.semaphore_wait(barrier, 5 + cols + at_wall * (rows * n_wrap * n_norm + 3))
-
-    @pl.when(normal == 0)
-    def _():
-        for one in wide:
-            one.start()
-
     first = stage_copies(0, field1)
     for one in first:
         one.start()
 
     for read in reads[2:]:
         read.wait()
+    for d in range(3):
+        for u in range(VARS):
+            for v in range(VARS):
+                scaled = jac_held[u, d, v] * (-1.0 / 12.0)
+                jac[25 * d + 5 * u + v] = jnp.full((8, LANES), scaled, jnp.float32)
     lane = lane_of((8, LANES))
     held = jnp.where(lane < LANES // 2, 2 * lane, 2 * lane - (LANES - 1))
 
-    def group_copy(buffer, slot, which, target):
+    def group_copy(buffer, own, which, target):
         return pltpu.make_async_remote_copy(
-            src_ref=buffer.at[0],
-            dst_ref=buffer.at[slot],
+            src_ref=buffer.at[own],
+            dst_ref=buffer.at[own],
             send_sem=group_sem.at[2 * which],
             recv_sem=group_sem.at[2 * which + 1],
             device_id=target,
             device_id_type=MESH,
         )
+
+    def added(ref):
+        terms = [ref[i] for i in range(ref.shape[0])]
+        while len(terms) > 1:
+            terms = [sum(terms[i + 1 : i + 2], terms[i]) for i in range(0, len(terms), 2)]
+        return terms[0]
 
     def take(ref, which):
         pltpu.make_async_copy(ref, ref, group_sem.at[which]).wait()
@@ -511,23 +561,20 @@
             faces[s] = jnp.where(place == aims, weight, 0.0)
         for one in wide:
             one.wait_recv()
-        loads_a[0] = wall_loads(
+        loads_a[y_own] = wall_loads(
             span,
             n_span,
             wall_packed,
             wall_beside,
-            wall_corner,
+            edge_got,
+            tip_got,
             wall_layer,
             wall_mid,
             faces,
             jac,
         )
-        for a in range(rows):
-            for b in range(n_wrap):
-                for c in range(n_norm):
-                    if a or b or c:
-                        target = (row_at[a] * cols + col, wrap_at[b], c)
-                        group_copy(loads_a, a * n_wrap + b, 0, target).start()
+        for k in range(1, len(y_at)):
+            group_copy(loads_a, y_own, 0, device(y_at[k], z, core, 0)).start()
 
     for one in first:
         one.wait_recv()
@@ -552,21 +599,17 @@
     @pl.when(normal == 0)
     def _():
         take(loads_a.at[1:], 1)
-
-    @pl.when(normal != 0)
-    def _():
-        take(loads_a, 1)
-
-    count_a = rows * n_wrap
-    total = None
-    for y in range(count_a):
-        a = (row + (rows - y // n_wrap)) % rows
-        b = (wrap + (n_wrap - y % n_wrap)) % n_wrap
-        term = loads_a[a * n_wrap + b]
-        total = term if total is None else total + term
-    loads_b[0] = total
-    for k in range(1, cols):
-        group_copy(loads_b, k, 1, (row * cols + col_at[k], wrap, normal)).start()
+        loads_b[z] = added(loads_a)
+        for k in range(1, zs):
+            group_copy(loads_b, z, 1, device(here, z_at[k], core, 0)).start()
+        if zs > 1:
+            take(loads_b.at[1:], 3)
+        loads_c[core] = added(loads_b)
+        for x in range(n_norm - 1, -1, -1):
+            for k in range(cores):
+                if x or k:
+                    group_copy(loads_c, core, 2, device(here, z, core_at[k], x)).start()
+
     for one in second:
         one.wait_recv()
     stage_arrive(1, field2)
@@ -582,61 +625,54 @@
 
     lax.fori_loop(0, SPAN, second_plane, 0)
 
-    write = pltpu.make_async_copy(result, out_hbm, local_sem.at[len(inputs)])
-    write.start()
-
-    take(loads_b.at[1:], 3)
-    total = None
-    for z in range(cols):
-        term = loads_b[(col + (cols - z)) % cols]
-        total = term if total is None else total + term
-    loads = jnp.sum(total, axis=0, keepdims=True)
+    for one in first + second:
+        one.wait_send()
+
+    @pl.when(normal == 0)
+    def _():
+        for one in wide:
+            one.wait_send()
+        take(loads_a.at[1:], 0)
+        if zs > 1:
+            take(loads_b.at[1:], 2)
+        take(tally, 4)
+
+    @pl.when(normal == 0)
+    def _():
+        take(loads_c.at[1:], 5)
+
+    @pl.when(normal != 0)
+    def _():
+        take(loads_c, 5)
+
+    loads = added(loads_c)
 
     le, lo = halves(loads)
     fe, fo = fe + le, fo + lo
-    ue, uo = substitute(factors, *right_side(fe, fo, he, ho, ue, uo))
-    for i, x in enumerate((be, bo, ge, go, he, ho, fe, fo, ue, uo)):
-        state_ref[i : i + 1, :] = x
-
-    for one in first + second:
-        one.wait_send()
-
-    @pl.when(normal == 0)
-    def _():
-        for one in wide:
-            one.wait_send()
-        take(tally, 0)
-
-    take(loads_b.at[1:], 2)
-    write.wait()
-
-
-def beam_kernel(state_ref, flow_hbm, out_hbm, defl_ref, held, read_sem, write_sem):
-    def each(src, dst, sem):
-        return [pltpu.make_async_copy(src.at[v], dst.at[v], sem.at[v]) for v in range(VARS)]
-
-    reads, writes = each(flow_hbm, held, read_sem), each(held, out_hbm, write_sem)
-    for read in reads:
-        read.start()
-    for read, write in zip(reads, writes):
-        read.wait()
-        write.start()
-    be, bo, ge, go, he, ho, fe, fo, ue, uo = [state_ref[i : i + 1, :] for i in range(10)]
-    for _ in range(NEWTON - 1):
-        factors = factor(be, bo, ge + 3.0 * he * ue * ue, go + 3.0 * ho * uo * uo)
+    for newton_step in range(NEWTON):
+        if newton_step:
+            factors = factor(be, bo, ge + 3.0 * he * ue * ue, go + 3.0 * ho * uo * uo)
         ue, uo = substitute(factors, *right_side(fe, fo, he, ho, ue, uo))
     both = jnp.where(lane_of((1, LANES)) < LANES // 2, ue, roll(uo, LANES // 2))
-    lane = lane_of((8, LANES))
     back = (lane % 2) * (LANES // 2) + lane // 2
     full = jnp.broadcast_to(both, (8, LANES))
     defl_ref[...] = jnp.take_along_axis(full, back, axis=1)[0:1]
-    for write in writes:
-        write.wait()
+
+
+def hand_out(flow_ref, defl_ref, flow_out, defl_out, sem):
+    copies = [
+        pltpu.make_async_copy(flow_ref, flow_out, sem.at[0]),
+        pltpu.make_async_copy(defl_ref, defl_out, sem.at[1]),
+    ]
+    for one in copies:
+        one.start()
+    for one in copies:
+        one.wait()
 
 
 def solution(mesh):
     n_span, n_wrap, n_norm = (mesh.shape[axis] for axis in ("span", "wrap", "normal"))
-    cols, ys = n_span // 2, 2 * n_wrap
+    zs, ys = n_span // 4, 2 * n_wrap
     f32 = jnp.float32
 
     def step(
@@ -655,15 +691,17 @@
         vectors = [
             x.reshape(1, STATIONS) for x in (contact, bending, mass, hardening, disp_old, vel_old)
         ]
-        hbm = pl.BlockSpec(memory_space=pltpu.HBM)
-        flow_next, state = pl.pallas_call(
+        hbm, vmem = (pl.BlockSpec(memory_space=space) for space in (pltpu.HBM, pltpu.VMEM))
+        operands = [flow_state, inv_volume, flux_jacobians.transpose(1, 0, 2), area, station_map]
+        operands = [pltpu.with_memory_space_constraint(x, pltpu.HBM) for x in operands + vectors]
+        flow_next, deflection = pl.pallas_call(
             functools.partial(kernel, n_span, n_wrap, n_norm),
             out_shape=(
-                jax.ShapeDtypeStruct(flow_state.shape, f32),
-                jax.ShapeDtypeStruct((16, LANES), f32),
+                pltpu.VMEM(flow_state.shape, f32),
+                pltpu.VMEM((1, STATIONS), f32),
             ),
-            in_specs=[hbm, hbm, pl.BlockSpec(memory_space=pltpu.SMEM)] + [hbm] * 8,
-            out_specs=(hbm, pl.BlockSpec(memory_space=pltpu.VMEM)),
+            in_specs=[hbm] * len(operands),
+            out_specs=(vmem, vmem),
             scratch_shapes=[
                 pltpu.VMEM((VARS, SPAN + 4, WRAP + 16, LANES), f32),
                 pltpu.VMEM((VARS, SPAN + 4, WRAP + 16, LANES), f32),
@@ -673,49 +711,52 @@
                 pltpu.VMEM((2, 3, VARS, 8, LANES), f32),
                 pltpu.VMEM((VARS, 8, LANES), f32),
                 pltpu.VMEM((75, 8, LANES), f32),
-                pltpu.VMEM((VARS, SPAN, WRAP, LANES), f32),
                 pltpu.VMEM((SPAN, WRAP, LANES), f32),
                 pltpu.VMEM((SPAN, WRAP), f32),
                 pltpu.VMEM((SPAN, WRAP), jnp.int32),
                 pltpu.VMEM((1, STATIONS), jnp.int32),
                 pltpu.VMEM((5, 1, STATIONS), f32),
-                pltpu.VMEM((ys, 8, LANES), f32),
-                pltpu.VMEM((cols, 8, LANES), f32),
-                pltpu.VMEM((ys * n_norm - 1, 8, LANES), f32),
+                pltpu.SMEM((VARS, 3, VARS), f32),
+                pltpu.VMEM((ys, 1, LANES), f32),
+                pltpu.VMEM((zs, 1, LANES), f32),
+                pltpu.VMEM((2, 1, LANES), f32),
+                pltpu.VMEM((2 * n_norm - 1, 1, LANES), f32),
                 pltpu.VMEM((VARS + 1, WRAP, LANES), f32),
-                pltpu.VMEM((4, VARS + 1, WRAP, LANES), f32),
-                pltpu.VMEM((4, VARS + 1, 8, LANES), f32),
+                pltpu.VMEM((3, WRAP, LANES), f32),
+                pltpu.VMEM((2, 3, WRAP, LANES), f32),
+                pltpu.VMEM((2, 2, 8, LANES), f32),
+                pltpu.VMEM((2, 2, 8, LANES), f32),
+                pltpu.VMEM((2, 8, LANES), f32),
+                pltpu.VMEM((4, 8, LANES), f32),
                 pltpu.VMEM((VARS + 1, WRAP + 16, LANES), f32),
                 pltpu.VMEM((VARS, 24, LANES), f32),
                 pltpu.SemaphoreType.DMA((11,)),
                 pltpu.SemaphoreType.DMA((12,)),
                 pltpu.SemaphoreType.DMA((12,)),
-                pltpu.SemaphoreType.DMA((4,)),
+                pltpu.SemaphoreType.DMA((6,)),
                 pltpu.SemaphoreType.DMA((8,)),
                 pltpu.SemaphoreType.DMA((8,)),
             ],
             compiler_params=pltpu.CompilerParams(
-                collective_id=0, has_side_effects=True, vmem_limit_bytes=60 * 1024 * 1024
+                collective_id=0, has_side_effects=True, vmem_limit_bytes=32 * 1024 * 1024
             ),
             cost_estimate=pl.CostEstimate(
                 flops=10_000_000, bytes_accessed=1_000_000, transcendentals=0
             ),
-        )(flow_state, inv_volume, flux_jacobians.transpose(1, 0, 2), area, station_map, *vectors)
+        )(*operands)
         flow_next, deflection = pl.pallas_call(
-            beam_kernel,
+            hand_out,
             out_shape=(
                 jax.ShapeDtypeStruct(flow_state.shape, f32),
                 jax.ShapeDtypeStruct((1, STATIONS), f32),
             ),
-            in_specs=[pl.BlockSpec(memory_space=pltpu.VMEM), hbm],
-            out_specs=(hbm, pl.BlockSpec(memory_space=pltpu.VMEM)),
-            scratch_shapes=[
-                pltpu.VMEM((VARS, SPAN, WRAP, LANES), f32),
-                pltpu.SemaphoreType.DMA((VARS,)),
-                pltpu.SemaphoreType.DMA((VARS,)),
-            ],
-            compiler_params=pltpu.CompilerParams(vmem_limit_bytes=60 * 1024 * 1024),
-        )(state, flow_next)
+            in_specs=(vmem, vmem),
+            out_specs=(hbm, hbm),
+            scratch_shapes=[pltpu.SemaphoreType.DMA((2,))],
+        )(
+            pltpu.with_memory_space_constraint(flow_next, pltpu.VMEM),
+            pltpu.with_memory_space_constraint(deflection, pltpu.VMEM),
+        )
         return flow_next, deflection.reshape(STATIONS)
 
     placed = (

time: 40.6 us -> 32.8 us (0.81)
  Pallas kernels: 39.6 us -> 32 us
    pallas_call x1, Pallas kernels: 36 us -> 31.3 us  [step(): pl.pallas_call(functools.partial(kernel, n_span, n_wrap, n_norm), out_sha...]
    pallas_call x1, Pallas kernels: 3.65 us -> 0.75 us  [step(): pl.pallas_call(hand_out, out_shape=(jax.ShapeDtypeStruct(flow_state.shape...]
where the time goes in v2:
time: 32.8 us; the launch traced here: 32.6 us
  Pallas kernels  32 us (98%)
  between operations  0.64 us (2%)
    pallas_call x1, Pallas kernels, step(): pl.pallas_call(functools.partial(kernel, n_span, n_wrap, n_norm), out_sha...  31.3 us
    pallas_call x1, Pallas kernels, step(): pl.pallas_call(hand_out, out_shape=(jax.ShapeDtypeStruct(flow_state.shape...  0.75 us

profile of v2, /device:TPU:1, one launch (start us, length us, event | category | flops | bytes accessed | tf_op | source)
XLA Modules:
  0.0 32.6 jit_solution(1402918059690517333)
XLA Ops:
  0.6 31.3 %shard_map.122 = (f32[5,8,16,128]{3,2,1,0:T(8,128)S(1)}, f32[1,128]{1,0:T(1,128)S(1)}) custom-call(f32[5,8,16,128]{3,2,1,0:T(8,128)} %flow_hbm.1, f32[8,16,128]{2,1,0:T(8,128)} %volume_hbm.1, f32[5,3,5]{2,1,0:T(4,128)} %bitcast.8, f32[8,16]{1,0:T(8,128)} %area_hbm.1, s32[8,16]{1,0:T(8,128)} %map_hbm.1, s32[1,128]{1,0:T(1,128)} %bitcast.9, ...), custom_call_target="tpu_custom_call" | custom-call | flops 10000000 | bytes 1000000 | tf_op jit(solution)/shard_map/pallas_call | solution.py:697
  31.9 0.7 %shard_map.123 = (f32[5,8,16,128]{3,2,1,0:T(8,128)}, f32[1,128]{1,0:T(1,128)}) custom-call(f32[5,8,16,128]{3,2,1,0:T(8,128)S(1)} %get-tuple-element.6.flow_ref, f32[1,128]{1,0:T(1,128)S(1)} %get-tuple-element.7.defl_ref), custom_call_target="tpu_custom_call" | custom-call | tf_op jit(solution)/shard_map/pallas_call | solution.py:747

commit v3 on v2

--- a/solution.py
+++ b/solution.py
@@ -45,35 +45,43 @@
     step = 1
     while step < half:
         inv = 1.0 / (p * r - q * q)
-        w11, w12, w22 = r * inv, -q * inv, p * inv
-        u11, u12 = c11 * w11 + c21 * w12, c11 * w12 + c21 * w22
-        u21, u22 = c12 * w11 + c22 * w12, c12 * w12 + c22 * w22
-        d11, d12 = a11 * w11 + a21 * w12, a11 * w12 + a21 * w22
-        d21, d22 = a12 * w11 + a22 * w12, a12 * w12 + a22 * w22
-        levels.append((step, u11, u12, u21, u22, d11, d12, d21, d22))
-        p = p - roll(u11 * c11 + u12 * c21, step) - roll(d11 * a11 + d12 * a21, -step)
-        q = q - roll(u11 * c12 + u12 * c22, step) - roll(d11 * a12 + d12 * a22, -step)
-        r = r - roll(u21 * c12 + u22 * c22, step) - roll(d21 * a12 + d22 * a22, -step)
+        u11, u12 = c11 * r - c21 * q, c21 * p - c11 * q
+        u21, u22 = c12 * r - c22 * q, c22 * p - c12 * q
+        d11, d12 = a11 * r - a21 * q, a21 * p - a11 * q
+        d21, d22 = a12 * r - a22 * q, a22 * p - a12 * q
+        levels.append((step, inv, u11, u12, u21, u22, d11, d12, d21, d22))
+        up = [
+            (u11 * c11 + u12 * c21) * inv,
+            (u11 * c12 + u12 * c22) * inv,
+            (u21 * c12 + u22 * c22) * inv,
+        ]
+        down = [
+            (d11 * a11 + d12 * a21) * inv,
+            (d11 * a12 + d12 * a22) * inv,
+            (d21 * a12 + d22 * a22) * inv,
+        ]
+        p = p - (roll(up[0], step) + roll(down[0], -step))
+        q = q - (roll(up[1], step) + roll(down[1], -step))
+        r = r - (roll(up[2], step) + roll(down[2], -step))
         if 2 * step < half:
-            n11, n12 = -(d11 * c11 + d12 * c21), -(d11 * c12 + d12 * c22)
-            n21, n22 = -(d21 * c11 + d22 * c21), -(d21 * c12 + d22 * c22)
+            n11, n12 = -(d11 * c11 + d12 * c21) * inv, -(d11 * c12 + d12 * c22) * inv
+            n21, n22 = -(d21 * c11 + d22 * c21) * inv, -(d21 * c12 + d22 * c22) * inv
             c11, c12 = roll(n11, -step), roll(n12, -step)
             c21, c22 = roll(n21, -step), roll(n22, -step)
             a11, a12 = roll(n11, step), roll(n21, step)
             a21, a22 = roll(n12, step), roll(n22, step)
         step *= 2
-    inv = 1.0 / (p * r - q * q)
-    return levels, (r * inv, -q * inv, p * inv)
+    return levels, (1.0 / (p * r - q * q), p, q, r)
 
 
 def substitute(factors, e, o):
-    levels, (w11, w12, w22) = factors
-    for step, u11, u12, u21, u22, d11, d12, d21, d22 in levels:
+    levels, (inv, p, q, r) = factors
+    for step, scale, u11, u12, u21, u22, d11, d12, d21, d22 in levels:
         e, o = (
-            e - roll(u11 * e + u12 * o, step) - roll(d11 * e + d12 * o, -step),
-            o - roll(u21 * e + u22 * o, step) - roll(d21 * e + d22 * o, -step),
+            e - (roll((u11 * e + u12 * o) * scale, step) + roll((d11 * e + d12 * o) * scale, -step)),
+            o - (roll((u21 * e + u22 * o) * scale, step) + roll((d21 * e + d22 * o) * scale, -step)),
         )
-    return w11 * e + w12 * o, w12 * e + w22 * o
+    return (r * e - q * o) * inv, (p * o - q * e) * inv
 
 
 def right_side(fe, fo, he, ho, ue, uo):
@@ -83,6 +91,10 @@
 def halves(x):
     valid = lane_of((1, LANES)) < LANES // 2
     return jnp.where(valid, x, 0.0), jnp.where(valid, roll(x, LANES // 2), 0.0)
+
+
+def ring(by, count):
+    return min(by, count - by)
 
 
 def pack_plane(packed, cells, s):
@@ -166,7 +178,7 @@
                 else:
                     tile = volume[s, 8 * t : 8 * t + 8, :]
                 have = jnp.where(group == s + 4, roll(tile, 8 * (s + 4) + 2), have)
-            packed[v, 8 * t : 8 * t + 8, :] = have
+            packed[v, 8 * t : 8 * t + 8, :] = mirrored(have)
 
 
 def pair_wall(packed, pairs, edge, tip):
@@ -198,7 +210,7 @@
     return jnp.where(place == 0, roll(x, -3), jnp.where(place == 1, roll(x, -1), x))
 
 
-def wall_rates(layer, top, rows, wanted, jac):
+def wall_rates(layer, top, rows, wanted, jac, at_wall):
     cells, grads, smooths = [], [[], [], []], []
     shape = (rows // 8, 8, LANES)
     for v in range(VARS):
@@ -206,8 +218,12 @@
         reads = [
             [roll(c, -8 * k) for k in (-2, -1, 1, 2)],
             [layer[v, top + k : top + k + rows, :] for k in (-2, -1, 1, 2)],
-            [roll(c, -k) for k in (-2, -1, 1, 2)],
-        ]
+        ]
+        if at_wall:
+            p1, p2 = roll(c, -1), roll(c, -2)
+            reads.append([p1, c, p1, p2])
+        else:
+            reads.append([roll(c, -k) for k in (-2, -1, 1, 2)])
         near, far = None, None
         for d, (m2, m1, p1, p2) in enumerate(reads):
             grads[d].append(((m2 - p2) + 8.0 * (p1 - m1)).reshape(shape))
@@ -246,14 +262,14 @@
             left = jnp.where(first, 0.0, swing(left, not upper))
             right = jnp.where(last, 0.0, swing(right, not upper))
             whole = jnp.where(group < 4, left, jnp.where(group >= 12, right, centre))
-            layer[v, 8 * t : 8 * t + 8, :] = mirrored(whole)
+            layer[v, 8 * t : 8 * t + 8, :] = whole
     span_group = lane_of((24, LANES)) // 8
     outside = (first & (span_group < 4)) | (last & (span_group >= 12))
-    cells, rates = wall_rates(layer, 4, 24, VARS, jac)
+    cells, rates = wall_rates(layer, 4, 24, VARS, jac, False)
     scale = DT_FLOW * layer[VARS, 4:28, :]
     for u in range(VARS):
-        mid[u] = mirrored(jnp.where(outside, 0.0, cells[u] + scale * rates[u]))
-    cells, rates = wall_rates(mid, 4, 16, 1, jac)
+        mid[u] = jnp.where(outside, 0.0, cells[u] + scale * rates[u])
+    cells, rates = wall_rates(mid, 4, 16, 1, jac, True)
     scale = DT_FLOW * layer[VARS, 8:24, :]
     after = 0.5 * (layer[0, 8:24, :] + cells[0] + scale * rates[0])
     total = jnp.zeros((WRAP, LANES), jnp.float32)
@@ -336,7 +352,7 @@
         (jac_hbm, jac_held),
     ]
     reads = [pltpu.make_async_copy(a, b, local_sem.at[i]) for i, (a, b) in enumerate(inputs)]
-    for read in reads:
+    for read in reads[:2]:
         read.start()
 
     def turned(index, by, count):
@@ -362,7 +378,6 @@
         pl.semaphore_signal(barrier, inc=1, device_id=target, device_id_type=MESH)
 
     corners = [(span_at[i], wrap_at[j], normal) for j in (n_wrap - 1, 1) for i in (-1, 1)]
-
     for side in sides:
         greet(side)
 
@@ -371,16 +386,18 @@
 
     here = (row, wrap)
     y_at = [(row_at[a], wrap_at[b]) for a in range(rows) for b in range(n_wrap)]
+    y_far = sorted(range(1, rows * n_wrap), key=lambda k: -ring(2 * (k % n_wrap) + k // n_wrap, 2 * n_wrap))
+    z_far = sorted(range(1, zs), key=lambda k: -ring(k, zs))
     beside_y = (1, n_wrap - 1)
 
     @pl.when(normal == 0)
     def _():
         for one in corners:
             greet(one)
-        for k in range(1, len(y_at)):
+        for k in y_far:
             if k not in beside_y:
                 greet(device(y_at[k], z, core, 0))
-        for k in range(1, zs):
+        for k in z_far:
             greet(device(here, z_at[k], core, 0))
 
     @pl.when(normal != 0)
@@ -479,6 +496,8 @@
         for one in wide:
             one.start()
 
+    for read in reads[2:]:
+        read.start()
     stage_wrap_rows(0, field1)
 
     def pack_first(s, packed):
@@ -573,7 +592,7 @@
             faces,
             jac,
         )
-        for k in range(1, len(y_at)):
+        for k in y_far:
             group_copy(loads_a, y_own, 0, device(y_at[k], z, core, 0)).start()
 
     for one in first:
@@ -600,12 +619,12 @@
     def _():
         take(loads_a.at[1:], 1)
         loads_b[z] = added(loads_a)
-        for k in range(1, zs):
+        for k in z_far:
             group_copy(loads_b, z, 1, device(here, z_at[k], core, 0)).start()
         if zs > 1:
             take(loads_b.at[1:], 3)
         loads_c[core] = added(loads_b)
-        for x in range(n_norm - 1, -1, -1):
+        for x in sorted(range(n_norm), key=lambda x: -ring(x, n_norm)):
             for k in range(cores):
                 if x or k:
                     group_copy(loads_c, core, 2, device(here, z, core_at[k], x)).start()

time: 32.8 us -> 32.5 us (level)
  Pallas kernels: 32 us -> 31.6 us
    pallas_call x1, Pallas kernels: 31.3 us -> 30.9 us  [step(): pl.pallas_call(functools.partial(kernel, n_span, n_wrap, n_norm), out_sha...]
where the time goes in v3:
time: 32.5 us; the launch traced here: 32.3 us
  Pallas kernels  31.6 us (97%)
  between operations  0.64 us (2%)
    pallas_call x1, Pallas kernels, step(): pl.pallas_call(functools.partial(kernel, n_span, n_wrap, n_norm), out_sha...  30.9 us
    pallas_call x1, Pallas kernels, step(): pl.pallas_call(hand_out, out_shape=(jax.ShapeDtypeStruct(flow_state.shape...  0.75 us

profile of v3, /device:TPU:1, one launch (start us, length us, event | category | flops | bytes accessed | tf_op | source)
XLA Modules:
  0.0 32.3 jit_solution(12990665741075233877)
XLA Ops:
  0.6 30.9 %shard_map.122 = (f32[5,8,16,128]{3,2,1,0:T(8,128)S(1)}, f32[1,128]{1,0:T(1,128)S(1)}) custom-call(f32[5,8,16,128]{3,2,1,0:T(8,128)} %flow_hbm.1, f32[8,16,128]{2,1,0:T(8,128)} %volume_hbm.1, f32[5,3,5]{2,1,0:T(4,128)} %bitcast.8, f32[8,16]{1,0:T(8,128)} %area_hbm.1, s32[8,16]{1,0:T(8,128)} %map_hbm.1, s32[1,128]{1,0:T(1,128)} %bitcast.9, ...), custom_call_target="tpu_custom_call" | custom-call | flops 10000000 | bytes 1000000 | tf_op jit(solution)/shard_map/pallas_call | solution.py:716
  31.5 0.7 %shard_map.123 = (f32[5,8,16,128]{3,2,1,0:T(8,128)}, f32[1,128]{1,0:T(1,128)}) custom-call(f32[5,8,16,128]{3,2,1,0:T(8,128)S(1)} %get-tuple-element.6.flow_ref, f32[1,128]{1,0:T(1,128)S(1)} %get-tuple-element.7.defl_ref), custom_call_target="tpu_custom_call" | custom-call | tf_op jit(solution)/shard_map/pallas_call | solution.py:766

commit v4 on v3

--- a/solution.py
+++ b/solution.py
@@ -130,9 +130,7 @@
         corr[u] = total
 
 
-def plane_rates(field, s, jac, corr):
-    lane = lane_of((8, LANES))
-    edge = (lane < 2) | (lane >= LANES - 2)
+def plane_rates(field, s, jac):
     cells, grads, smooths = [], [[], [], []], []
     for v in range(VARS):
 
@@ -158,13 +156,73 @@
         for d in range(3):
             for v in range(VARS):
                 total = total + jac[25 * d + 5 * u + v][None] * grads[d][v]
-        ends = corr[u]
-        fix = [
-            jnp.where(edge, roll(ends, (2 * LANES - 2 - 4 * (2 * s + t)) % LANES), 0.0)
-            for t in range(2)
-        ]
-        rates.append(total + jnp.stack(fix))
+        rates.append(total)
     return cells, rates
+
+
+def ghost_rates(direction, low, first, second, jac, shape):
+    outer, inner = [], []
+    for v in range(VARS):
+        a, b = first(v), second(v)
+        if low:
+            outer.append((a - 8.0 * b, a - 4.0 * b))
+            inner.append((b, b))
+        else:
+            outer.append((8.0 * a - b, b - 4.0 * a))
+            inner.append((-a, a))
+    fixes = []
+    for layer in (outer, inner):
+        grads = [g.reshape(shape) for g, _ in layer]
+        layer_fixes = []
+        for u in range(VARS):
+            total = -DISSIPATION * layer[u][1].reshape(shape)
+            for v in range(VARS):
+                total = total + jac[25 * direction + 5 * u + v][None] * grads[v]
+            layer_fixes.append(total)
+        fixes.append(layer_fixes)
+    return fixes
+
+
+def add_ghosts(span, n_span, planes, rows, corr, jac, volume, factor_of, at_plane, at_row, at_cells, done):
+    for low in (True, False):
+        gone = span == (0 if low else n_span - 1)
+        side = 0 if low else 1
+
+        def ghost(layer):
+            return lambda v: jnp.where(gone, 0.0, planes[side, v, layer])
+
+        fixes = ghost_rates(0, low, ghost(0), ghost(1), jac, (2, 8, LANES))
+        for s, fix in zip((0, 1) if low else (SPAN - 1, SPAN - 2), fixes):
+            scale = factor_of * volume[s]
+            for u in range(VARS):
+                at_plane(u, s, scale * fix[u].reshape(WRAP, LANES))
+    for low in (True, False):
+        side = 1 if low else 0
+
+        def ghost(layer):
+            return lambda v: rows[side, v, layer]
+
+        fixes = ghost_rates(1, low, ghost(0), ghost(1), jac, (1, 8, LANES))
+        for r, fix in zip((0, 1) if low else (WRAP - 1, WRAP - 2), fixes):
+            scale = factor_of * volume[:, r, :]
+            for u in range(VARS):
+                at_row(u, r, scale * fix[u].reshape(8, LANES))
+    lane = lane_of((8, LANES))
+    edge = (lane < 2) | (lane >= LANES - 2)
+
+    def columns(s, carry):
+        scale = factor_of * volume[s].reshape(2, 8, LANES)
+        cells = []
+        for u in range(VARS):
+            ends = corr[u]
+            fix = [
+                jnp.where(edge, roll(ends, (2 * LANES - 2 - 4 * (2 * s + t)) % LANES), 0.0)
+                for t in range(2)
+            ]
+            cells.append(at_cells(u, s, scale * jnp.stack(fix)))
+        return done(carry, cells, s)
+
+    return columns
 
 
 def pack_wall(field, volume, packed):
@@ -298,6 +356,7 @@
     defl_ref,
     field1,
     field2,
+    planes,
     volume,
     wall_send,
     wall_recv,
@@ -419,8 +478,8 @@
         cells = pl.ds(TOP, WRAP)
         base = 6 * stage
         pairs = [
-            (field.at[:, 2:4, cells, :], field.at[:, 2 + SPAN : 4 + SPAN, cells, :]),
-            (field.at[:, SPAN : 2 + SPAN, cells, :], field.at[:, 0:2, cells, :]),
+            (field.at[:, 2:4, cells, :], planes.at[stage, 1]),
+            (field.at[:, SPAN : 2 + SPAN, cells, :], planes.at[stage, 0]),
             (wall_send.at[stage, 0], wall_recv.at[stage, 0]),
             (wall_send.at[stage, 1], wall_recv.at[stage, 1]),
             (edges.at[stage, 0], edges.at[stage, 2]),
@@ -434,24 +493,16 @@
                 wall_send[stage, 0, v, r] = field[v, 2 : 2 + SPAN, TOP + r, :]
                 wall_send[stage, 1, v, r] = field[v, 2 : 2 + SPAN, TOP + WRAP - 2 + r, :]
 
-    def stage_arrive(stage, field):
-        zeros = jnp.zeros((VARS, 2, WRAP, LANES), jnp.float32)
-
-        @pl.when(span == 0)
-        def _():
-            field[:, 0:2, TOP : TOP + WRAP, :] = zeros
-
-        @pl.when(span == n_span - 1)
-        def _():
-            field[:, 2 + SPAN : 4 + SPAN, TOP : TOP + WRAP, :] = zeros
-
-        for v in range(VARS):
-            for r in range(2):
-                field[v, 2 : 2 + SPAN, TOP + WRAP + r, :] = wall_recv[stage, 0, v, r]
-                field[v, 2 : 2 + SPAN, TOP - 2 + r, :] = wall_recv[stage, 1, v, r]
+    def stage_columns(stage):
         edge_terms(
             normal, n_norm, edges.at[stage, 0], edges.at[stage, 1], edges.at[stage, 2], jac, corr
         )
+
+    for field in (field1, field2):
+        for s in (0, 1, 2 + SPAN, 3 + SPAN):
+            field[:, s, TOP : TOP + WRAP, :] = jnp.zeros((VARS, WRAP, LANES), jnp.float32)
+        for r in (0, TOP + WRAP):
+            field[:, 2 : 2 + SPAN, r : r + 8, :] = jnp.zeros((VARS, SPAN, 8, LANES), jnp.float32)
 
     wide = []
     for i, (src, dst, target) in enumerate(
@@ -543,23 +594,15 @@
     def take(ref, which):
         pltpu.make_async_copy(ref, ref, group_sem.at[which]).wait()
 
-    def permuted(x):
-        full = jnp.broadcast_to(x, (8, LANES))
-        return jnp.take_along_axis(full, held, axis=1)[0:1]
-
-    bending, mass, hardening, disp, vel = [permuted(beam_v[i]) for i in range(5)]
-    contact = permuted(contact_v[...])
-    inertia = 2.0 * mass / (DT_BEAM * DT_BEAM)
-    pull = CONTACT_STIFF * STOP_GAP
-    push = jnp.where(contact == 1, pull, jnp.where(contact == 2, -pull, 0.0))
-    steady = inertia * (disp + DT_BEAM * vel) + push
-    base = inertia + jnp.where(contact > 0, CONTACT_STIFF, 0.0)
-    be, bo = halves(bending)
-    he, ho = halves(hardening)
-    ge, go = halves(base)
-    ue, uo = halves(disp)
-    fe, fo = halves(steady)
-    factors = factor(be, bo, ge + 3.0 * he * ue * ue, go + 3.0 * ho * uo * uo)
+    def first_plane(s, carry):
+        cells, rates = plane_rates(field1, s, jac)
+        scale = DT_FLOW * volume[s].reshape(2, 8, LANES)
+        for u in range(VARS):
+            mid = cells[u] + scale * rates[u]
+            field2[u, s + 2, TOP : TOP + WRAP, :] = mid.reshape(WRAP, LANES)
+        return carry
+
+    lax.fori_loop(0, SPAN, first_plane, 0)
 
     @pl.when(normal == 0)
     def _():
@@ -597,17 +640,34 @@
 
     for one in first:
         one.wait_recv()
-    stage_arrive(0, field1)
-
-    def first_plane(s, packed):
-        cells, rates = plane_rates(field1, s, jac, corr)
-        scale = DT_FLOW * volume[s].reshape(2, 8, LANES)
-        mids = [cells[u] + scale * rates[u] for u in range(VARS)]
-        for u in range(VARS):
-            field2[u, s + 2, TOP : TOP + WRAP, :] = mids[u].reshape(WRAP, LANES)
-        return pack_plane(packed, mids, s)
-
-    packed = lax.fori_loop(0, SPAN, first_plane, empty)
+    stage_columns(0)
+
+    def mid_plane(u, s, part):
+        field2[u, s + 2, TOP : TOP + WRAP, :] += part
+
+    def mid_row(u, r, part):
+        field2[u, 2 : 2 + SPAN, TOP + r, :] += part
+
+    def mid_cells(u, s, part):
+        cells = field2[u, s + 2, TOP : TOP + WRAP, :].reshape(2, 8, LANES) + part
+        field2[u, s + 2, TOP : TOP + WRAP, :] = cells.reshape(WRAP, LANES)
+        return cells
+
+    columns = add_ghosts(
+        span,
+        n_span,
+        planes.at[0],
+        wall_recv.at[0],
+        corr,
+        jac,
+        volume,
+        DT_FLOW,
+        mid_plane,
+        mid_row,
+        mid_cells,
+        pack_plane,
+    )
+    packed = lax.fori_loop(0, SPAN, lambda s, packed: columns(s, packed), empty, unroll=True)
     for v in range(VARS):
         edges[1, 0, v] = packed[v]
 
@@ -615,12 +675,44 @@
     second = stage_copies(1, field2)
     for one in second:
         one.start()
+
+    def permuted(x):
+        full = jnp.broadcast_to(x, (8, LANES))
+        return jnp.take_along_axis(full, held, axis=1)[0:1]
+
+    bending, mass, hardening, disp, vel = [permuted(beam_v[i]) for i in range(5)]
+    contact = permuted(contact_v[...])
+    inertia = 2.0 * mass / (DT_BEAM * DT_BEAM)
+    pull = CONTACT_STIFF * STOP_GAP
+    push = jnp.where(contact == 1, pull, jnp.where(contact == 2, -pull, 0.0))
+    steady = inertia * (disp + DT_BEAM * vel) + push
+    base = inertia + jnp.where(contact > 0, CONTACT_STIFF, 0.0)
+    be, bo = halves(bending)
+    he, ho = halves(hardening)
+    ge, go = halves(base)
+    ue, uo = halves(disp)
+    fe, fo = halves(steady)
+    factors = factor(be, bo, ge + 3.0 * he * ue * ue, go + 3.0 * ho * uo * uo)
     @pl.when(normal == 0)
     def _():
         take(loads_a.at[1:], 1)
         loads_b[z] = added(loads_a)
         for k in z_far:
             group_copy(loads_b, z, 1, device(here, z_at[k], core, 0)).start()
+
+    def second_plane(s, carry):
+        cells, rates = plane_rates(field2, s, jac)
+        scale = DT_FLOW * volume[s].reshape(2, 8, LANES)
+        for u in range(VARS):
+            start = field1[u, s + 2, TOP : TOP + WRAP, :].reshape(2, 8, LANES)
+            after = 0.5 * (start + cells[u] + scale * rates[u])
+            result[u, s] = after.reshape(WRAP, LANES)
+        return carry
+
+    lax.fori_loop(0, SPAN, second_plane, 0)
+
+    @pl.when(normal == 0)
+    def _():
         if zs > 1:
             take(loads_b.at[1:], 3)
         loads_c[core] = added(loads_b)
@@ -631,18 +723,32 @@
 
     for one in second:
         one.wait_recv()
-    stage_arrive(1, field2)
-
-    def second_plane(s, carry):
-        cells, rates = plane_rates(field2, s, jac, corr)
-        scale = DT_FLOW * volume[s].reshape(2, 8, LANES)
-        for u in range(VARS):
-            start = field1[u, s + 2, TOP : TOP + WRAP, :].reshape(2, 8, LANES)
-            after = 0.5 * (start + cells[u] + scale * rates[u])
-            result[u, s] = after.reshape(WRAP, LANES)
-        return carry
-
-    lax.fori_loop(0, SPAN, second_plane, 0)
+    stage_columns(1)
+
+    def end_plane(u, s, part):
+        result[u, s] += part
+
+    def end_row(u, r, part):
+        result[u, :, r, :] += part
+
+    def end_cells(u, s, part):
+        result[u, s] += part.reshape(WRAP, LANES)
+
+    columns = add_ghosts(
+        span,
+        n_span,
+        planes.at[1],
+        wall_recv.at[1],
+        corr,
+        jac,
+        volume,
+        0.5 * DT_FLOW,
+        end_plane,
+        end_row,
+        end_cells,
+        lambda carry, cells, s: carry,
+    )
+    lax.fori_loop(0, SPAN, columns, 0, unroll=True)
 
     for one in first + second:
         one.wait_send()
@@ -724,6 +830,7 @@
             scratch_shapes=[
                 pltpu.VMEM((VARS, SPAN + 4, WRAP + 16, LANES), f32),
                 pltpu.VMEM((VARS, SPAN + 4, WRAP + 16, LANES), f32),
+                pltpu.VMEM((2, 2, VARS, 2, WRAP, LANES), f32),
                 pltpu.VMEM((SPAN, WRAP, LANES), f32),
                 pltpu.VMEM((2, 2, VARS, 2, SPAN, LANES), f32),
                 pltpu.VMEM((2, 2, VARS, 2, SPAN, LANES), f32),

time: 32.5 us -> 32.5 us (level)
  no operation moved by 1% of the time
where the time goes in v4:
time: 32.5 us; the launch traced here: 32.3 us
  Pallas kernels  31.7 us (98%)
  between operations  0.64 us (2%)
    pallas_call x1, Pallas kernels, step(): pl.pallas_call(functools.partial(kernel, n_span, n_wrap, n_norm), out_sha...  30.9 us
    pallas_call x1, Pallas kernels, step(): pl.pallas_call(hand_out, out_shape=(jax.ShapeDtypeStruct(flow_state.shape...  0.75 us

profile of v4, /device:TPU:1, one launch (start us, length us, event | category | flops | bytes accessed | tf_op | source)
XLA Modules:
  0.0 32.3 jit_solution(7585629048375625833)
XLA Ops:
  0.6 30.9 %shard_map.122 = (f32[5,8,16,128]{3,2,1,0:T(8,128)S(1)}, f32[1,128]{1,0:T(1,128)S(1)}) custom-call(f32[5,8,16,128]{3,2,1,0:T(8,128)} %flow_hbm.1, f32[8,16,128]{2,1,0:T(8,128)} %volume_hbm.1, f32[5,3,5]{2,1,0:T(4,128)} %bitcast.8, f32[8,16]{1,0:T(8,128)} %area_hbm.1, s32[8,16]{1,0:T(8,128)} %map_hbm.1, s32[1,128]{1,0:T(1,128)} %bitcast.9, ...), custom_call_target="tpu_custom_call" | custom-call | flops 10000000 | bytes 1000000 | tf_op jit(solution)/shard_map/pallas_call | solution.py:822
  31.6 0.7 %shard_map.123 = (f32[5,8,16,128]{3,2,1,0:T(8,128)}, f32[1,128]{1,0:T(1,128)}) custom-call(f32[5,8,16,128]{3,2,1,0:T(8,128)S(1)} %get-tuple-element.6.flow_ref, f32[1,128]{1,0:T(1,128)S(1)} %get-tuple-element.7.defl_ref), custom_call_target="tpu_custom_call" | custom-call | tf_op jit(solution)/shard_map/pallas_call | solution.py:873

commit v5 on v4

--- a/solution.py
+++ b/solution.py
@@ -437,8 +437,6 @@
         pl.semaphore_signal(barrier, inc=1, device_id=target, device_id_type=MESH)
 
     corners = [(span_at[i], wrap_at[j], normal) for j in (n_wrap - 1, 1) for i in (-1, 1)]
-    for side in sides:
-        greet(side)
 
     def device(y, z, core, x):
         return (y[0] * cols + z * cores + core, y[1], x)
@@ -451,18 +449,24 @@
 
     @pl.when(normal == 0)
     def _():
-        for one in corners:
-            greet(one)
+        for k in z_far:
+            greet(device(here, z_at[k], core, 0))
         for k in y_far:
             if k not in beside_y:
                 greet(device(y_at[k], z, core, 0))
-        for k in z_far:
-            greet(device(here, z_at[k], core, 0))
+        for one in corners:
+            greet(one)
 
     @pl.when(normal != 0)
     def _():
         for k in range(cores):
             greet(device(here, z, core_at[k], 0))
+
+    for side in sides:
+        greet(side)
+
+    for read in reads[2:]:
+        read.start()
 
     def copy(src, dst, slot, target):
         return pltpu.make_async_remote_copy(
@@ -538,17 +542,6 @@
         pack_wall(field1, volume, wall_packed)
         pair_wall(wall_packed, wall_pairs, edge_put, tip_put)
 
-    at_wall = lax.div(n_norm - normal, n_norm)
-    wall_peers = 4 + (len(y_at) - 1 - len(set(beside_y))) + (zs - 1) + cores * (n_norm - 1)
-    pl.semaphore_wait(barrier, 6 + at_wall * wall_peers)
-
-    @pl.when(normal == 0)
-    def _():
-        for one in wide:
-            one.start()
-
-    for read in reads[2:]:
-        read.start()
     stage_wrap_rows(0, field1)
 
     def pack_first(s, packed):
@@ -561,19 +554,64 @@
     for v in range(VARS):
         edges[0, 0, v] = packed[v]
 
-    first = stage_copies(0, field1)
-    for one in first:
-        one.start()
-
     for read in reads[2:]:
         read.wait()
+    lane = lane_of((8, LANES))
+    held = jnp.where(lane < LANES // 2, 2 * lane, 2 * lane - (LANES - 1))
+
     for d in range(3):
         for u in range(VARS):
             for v in range(VARS):
                 scaled = jac_held[u, d, v] * (-1.0 / 12.0)
                 jac[25 * d + 5 * u + v] = jnp.full((8, LANES), scaled, jnp.float32)
-    lane = lane_of((8, LANES))
-    held = jnp.where(lane < LANES // 2, 2 * lane, 2 * lane - (LANES - 1))
+    def permuted(x):
+        full = jnp.broadcast_to(x, (8, LANES))
+        return jnp.take_along_axis(full, held, axis=1)[0:1]
+
+    bending, mass, hardening, disp, vel = [permuted(beam_v[i]) for i in range(5)]
+    contact = permuted(contact_v[...])
+    inertia = 2.0 * mass / (DT_BEAM * DT_BEAM)
+    pull = CONTACT_STIFF * STOP_GAP
+    push = jnp.where(contact == 1, pull, jnp.where(contact == 2, -pull, 0.0))
+    steady = inertia * (disp + DT_BEAM * vel) + push
+    base = inertia + jnp.where(contact > 0, CONTACT_STIFF, 0.0)
+    be, bo = halves(bending)
+    he, ho = halves(hardening)
+    ge, go = halves(base)
+    ue, uo = halves(disp)
+    fe, fo = halves(steady)
+    factors = factor(be, bo, ge + 3.0 * he * ue * ue, go + 3.0 * ho * uo * uo)
+
+    @pl.when(normal == 0)
+    def _():
+        row_id = lax.broadcasted_iota(jnp.int32, (WRAP, WRAP), 0)
+        same = (row_id == lane_of((WRAP, WRAP))).astype(jnp.float32)
+
+        def turned_over(x):
+            return lax.dot_general(
+                same, x, (((1,), (1,)), ((), ())), precision=lax.Precision.HIGHEST
+            )
+
+        weights = turned_over(area[...])
+        places = turned_over(stations[...].astype(jnp.float32))
+        aims = jnp.broadcast_to(held[0:1], (WRAP, LANES)).astype(jnp.float32)
+        for s in range(SPAN):
+            weight = jnp.broadcast_to(weights[:, s : s + 1], (WRAP, LANES))
+            place = jnp.broadcast_to(places[:, s : s + 1], (WRAP, LANES))
+            faces[s] = jnp.where(place == aims, weight, 0.0)
+
+    at_wall = lax.div(n_norm - normal, n_norm)
+    wall_peers = 4 + (len(y_at) - 1 - len(set(beside_y))) + (zs - 1) + cores * (n_norm - 1)
+    pl.semaphore_wait(barrier, 6 + at_wall * wall_peers)
+
+    @pl.when(normal == 0)
+    def _():
+        for one in wide:
+            one.start()
+
+    first = stage_copies(0, field1)
+    for one in first:
+        one.start()
 
     def group_copy(buffer, own, which, target):
         return pltpu.make_async_remote_copy(
@@ -606,21 +644,6 @@
 
     @pl.when(normal == 0)
     def _():
-        row_id = lax.broadcasted_iota(jnp.int32, (WRAP, WRAP), 0)
-        same = (row_id == lane_of((WRAP, WRAP))).astype(jnp.float32)
-
-        def turned_over(x):
-            return lax.dot_general(
-                same, x, (((1,), (1,)), ((), ())), precision=lax.Precision.HIGHEST
-            )
-
-        weights = turned_over(area[...])
-        places = turned_over(stations[...].astype(jnp.float32))
-        aims = jnp.broadcast_to(held[0:1], (WRAP, LANES)).astype(jnp.float32)
-        for s in range(SPAN):
-            weight = jnp.broadcast_to(weights[:, s : s + 1], (WRAP, LANES))
-            place = jnp.broadcast_to(places[:, s : s + 1], (WRAP, LANES))
-            faces[s] = jnp.where(place == aims, weight, 0.0)
         for one in wide:
             one.wait_recv()
         loads_a[y_own] = wall_loads(
@@ -676,23 +699,6 @@
     for one in second:
         one.start()
 
-    def permuted(x):
-        full = jnp.broadcast_to(x, (8, LANES))
-        return jnp.take_along_axis(full, held, axis=1)[0:1]
-
-    bending, mass, hardening, disp, vel = [permuted(beam_v[i]) for i in range(5)]
-    contact = permuted(contact_v[...])
-    inertia = 2.0 * mass / (DT_BEAM * DT_BEAM)
-    pull = CONTACT_STIFF * STOP_GAP
-    push = jnp.where(contact == 1, pull, jnp.where(contact == 2, -pull, 0.0))
-    steady = inertia * (disp + DT_BEAM * vel) + push
-    base = inertia + jnp.where(contact > 0, CONTACT_STIFF, 0.0)
-    be, bo = halves(bending)
-    he, ho = halves(hardening)
-    ge, go = halves(base)
-    ue, uo = halves(disp)
-    fe, fo = halves(steady)
-    factors = factor(be, bo, ge + 3.0 * he * ue * ue, go + 3.0 * ho * uo * uo)
     @pl.when(normal == 0)
     def _():
         take(loads_a.at[1:], 1)

time: 32.5 us -> 32.5 us (level)
  no operation moved by 1% of the time
where the time goes in v5:
time: 32.5 us; the launch traced here: 32.4 us
  Pallas kernels  31.8 us (98%)
  between operations  0.64 us (2%)
    pallas_call x1, Pallas kernels, step(): pl.pallas_call(functools.partial(kernel, n_span, n_wrap, n_norm), out_sha...  31 us
    pallas_call x1, Pallas kernels, step(): pl.pallas_call(hand_out, out_shape=(jax.ShapeDtypeStruct(flow_state.shape...  0.75 us

profile of v5, /device:TPU:1, one launch (start us, length us, event | category | flops | bytes accessed | tf_op | source)
XLA Modules:
  0.0 32.4 jit_solution(18115548866753151992)
XLA Ops:
  0.6 31.0 %shard_map.122 = (f32[5,8,16,128]{3,2,1,0:T(8,128)S(1)}, f32[1,128]{1,0:T(1,128)S(1)}) custom-call(f32[5,8,16,128]{3,2,1,0:T(8,128)} %flow_hbm.1, f32[8,16,128]{2,1,0:T(8,128)} %volume_hbm.1, f32[5,3,5]{2,1,0:T(4,128)} %bitcast.8, f32[8,16]{1,0:T(8,128)} %area_hbm.1, s32[8,16]{1,0:T(8,128)} %map_hbm.1, s32[1,128]{1,0:T(1,128)} %bitcast.9, ...), custom_call_target="tpu_custom_call" | custom-call | flops 10000000 | bytes 1000000 | tf_op jit(solution)/shard_map/pallas_call | solution.py:828
  31.7 0.7 %shard_map.123 = (f32[5,8,16,128]{3,2,1,0:T(8,128)}, f32[1,128]{1,0:T(1,128)}) custom-call(f32[5,8,16,128]{3,2,1,0:T(8,128)S(1)} %get-tuple-element.6.flow_ref, f32[1,128]{1,0:T(1,128)S(1)} %get-tuple-element.7.defl_ref), custom_call_target="tpu_custom_call" | custom-call | tf_op jit(solution)/shard_map/pallas_call | solution.py:879

commit v6 on v5

--- a/solution.py
+++ b/solution.py
@@ -554,36 +554,21 @@
     for v in range(VARS):
         edges[0, 0, v] = packed[v]
 
-    for read in reads[2:]:
-        read.wait()
     lane = lane_of((8, LANES))
     held = jnp.where(lane < LANES // 2, 2 * lane, 2 * lane - (LANES - 1))
 
-    for d in range(3):
-        for u in range(VARS):
-            for v in range(VARS):
-                scaled = jac_held[u, d, v] * (-1.0 / 12.0)
-                jac[25 * d + 5 * u + v] = jnp.full((8, LANES), scaled, jnp.float32)
-    def permuted(x):
-        full = jnp.broadcast_to(x, (8, LANES))
-        return jnp.take_along_axis(full, held, axis=1)[0:1]
-
-    bending, mass, hardening, disp, vel = [permuted(beam_v[i]) for i in range(5)]
-    contact = permuted(contact_v[...])
-    inertia = 2.0 * mass / (DT_BEAM * DT_BEAM)
-    pull = CONTACT_STIFF * STOP_GAP
-    push = jnp.where(contact == 1, pull, jnp.where(contact == 2, -pull, 0.0))
-    steady = inertia * (disp + DT_BEAM * vel) + push
-    base = inertia + jnp.where(contact > 0, CONTACT_STIFF, 0.0)
-    be, bo = halves(bending)
-    he, ho = halves(hardening)
-    ge, go = halves(base)
-    ue, uo = halves(disp)
-    fe, fo = halves(steady)
-    factors = factor(be, bo, ge + 3.0 * he * ue * ue, go + 3.0 * ho * uo * uo)
+    def prepare():
+        for read in reads[2:]:
+            read.wait()
+        for d in range(3):
+            for u in range(VARS):
+                for v in range(VARS):
+                    scaled = jac_held[u, d, v] * (-1.0 / 12.0)
+                    jac[25 * d + 5 * u + v] = jnp.full((8, LANES), scaled, jnp.float32)
 
     @pl.when(normal == 0)
     def _():
+        prepare()
         row_id = lax.broadcasted_iota(jnp.int32, (WRAP, WRAP), 0)
         same = (row_id == lane_of((WRAP, WRAP))).astype(jnp.float32)
 
@@ -612,6 +597,11 @@
     first = stage_copies(0, field1)
     for one in first:
         one.start()
+
+    @pl.when(normal != 0)
+    def _():
+        prepare()
+
 
     def group_copy(buffer, own, which, target):
         return pltpu.make_async_remote_copy(
@@ -660,6 +650,10 @@
         )
         for k in y_far:
             group_copy(loads_a, y_own, 0, device(y_at[k], z, core, 0)).start()
+        take(loads_a.at[1:], 1)
+        loads_b[z] = added(loads_a)
+        for k in z_far:
+            group_copy(loads_b, z, 1, device(here, z_at[k], core, 0)).start()
 
     for one in first:
         one.wait_recv()
@@ -699,12 +693,16 @@
     for one in second:
         one.start()
 
+
     @pl.when(normal == 0)
     def _():
-        take(loads_a.at[1:], 1)
-        loads_b[z] = added(loads_a)
-        for k in z_far:
-            group_copy(loads_b, z, 1, device(here, z_at[k], core, 0)).start()
+        if zs > 1:
+            take(loads_b.at[1:], 3)
+        loads_c[core] = added(loads_b)
+        for x in sorted(range(n_norm), key=lambda x: -ring(x, n_norm)):
+            for k in range(cores):
+                if x or k:
+                    group_copy(loads_c, core, 2, device(here, z, core_at[k], x)).start()
 
     def second_plane(s, carry):
         cells, rates = plane_rates(field2, s, jac)
@@ -717,15 +715,23 @@
 
     lax.fori_loop(0, SPAN, second_plane, 0)
 
-    @pl.when(normal == 0)
-    def _():
-        if zs > 1:
-            take(loads_b.at[1:], 3)
-        loads_c[core] = added(loads_b)
-        for x in sorted(range(n_norm), key=lambda x: -ring(x, n_norm)):
-            for k in range(cores):
-                if x or k:
-                    group_copy(loads_c, core, 2, device(here, z, core_at[k], x)).start()
+    def permuted(x):
+        full = jnp.broadcast_to(x, (8, LANES))
+        return jnp.take_along_axis(full, held, axis=1)[0:1]
+
+    bending, mass, hardening, disp, vel = [permuted(beam_v[i]) for i in range(5)]
+    contact = permuted(contact_v[...])
+    inertia = 2.0 * mass / (DT_BEAM * DT_BEAM)
+    pull = CONTACT_STIFF * STOP_GAP
+    push = jnp.where(contact == 1, pull, jnp.where(contact == 2, -pull, 0.0))
+    steady = inertia * (disp + DT_BEAM * vel) + push
+    base = inertia + jnp.where(contact > 0, CONTACT_STIFF, 0.0)
+    be, bo = halves(bending)
+    he, ho = halves(hardening)
+    ge, go = halves(base)
+    ue, uo = halves(disp)
+    fe, fo = halves(steady)
+    factors = factor(be, bo, ge + 3.0 * he * ue * ue, go + 3.0 * ho * uo * uo)
 
     for one in second:
         one.wait_recv()

time: 32.5 us -> 33.1 us (1.018); the launches traced: 32.4 us -> 32.4 us
  no operation moved by 1% of the time
where the time goes in v6:
time: 33.1 us; the launch traced here: 32.4 us
  Pallas kernels  31.8 us (96%)
  between operations  0.64 us (2%)
    pallas_call x1, Pallas kernels, step(): pl.pallas_call(functools.partial(kernel, n_span, n_wrap, n_norm), out_sha...  31 us
    pallas_call x1, Pallas kernels, step(): pl.pallas_call(hand_out, out_shape=(jax.ShapeDtypeStruct(flow_state.shape...  0.75 us

profile of v6, /device:TPU:1, one launch (start us, length us, event | category | flops | bytes accessed | tf_op | source)
XLA Modules:
  0.0 32.4 jit_solution(6399664355288874721)
XLA Ops:
  0.6 31.0 %shard_map.122 = (f32[5,8,16,128]{3,2,1,0:T(8,128)S(1)}, f32[1,128]{1,0:T(1,128)S(1)}) custom-call(f32[5,8,16,128]{3,2,1,0:T(8,128)} %flow_hbm.1, f32[8,16,128]{2,1,0:T(8,128)} %volume_hbm.1, f32[5,3,5]{2,1,0:T(4,128)} %bitcast.8, f32[8,16]{1,0:T(8,128)} %area_hbm.1, s32[8,16]{1,0:T(8,128)} %map_hbm.1, s32[1,128]{1,0:T(1,128)} %bitcast.9, ...), custom_call_target="tpu_custom_call" | custom-call | flops 10000000 | bytes 1000000 | tf_op jit(solution)/shard_map/pallas_call | solution.py:834
  31.7 0.7 %shard_map.123 = (f32[5,8,16,128]{3,2,1,0:T(8,128)}, f32[1,128]{1,0:T(1,128)}) custom-call(f32[5,8,16,128]{3,2,1,0:T(8,128)S(1)} %get-tuple-element.6.flow_ref, f32[1,128]{1,0:T(1,128)S(1)} %get-tuple-element.7.defl_ref), custom_call_target="tpu_custom_call" | custom-call | tf_op jit(solution)/shard_map/pallas_call | solution.py:885

commit v7 on v6

--- a/solution.py
+++ b/solution.py
@@ -371,7 +371,6 @@
     jac_held,
     loads_a,
     loads_b,
-    loads_c,
     tally,
     wall_packed,
     wall_pairs,
@@ -450,7 +449,8 @@
     @pl.when(normal == 0)
     def _():
         for k in z_far:
-            greet(device(here, z_at[k], core, 0))
+            for c in range(cores):
+                greet(device(here, z_at[k], core_at[c], 0))
         for k in y_far:
             if k not in beside_y:
                 greet(device(y_at[k], z, core, 0))
@@ -459,8 +459,8 @@
 
     @pl.when(normal != 0)
     def _():
-        for k in range(cores):
-            greet(device(here, z, core_at[k], 0))
+        for k in y_far + [0]:
+            greet(device(y_at[k], z, core, 0))
 
     for side in sides:
         greet(side)
@@ -586,7 +586,7 @@
             faces[s] = jnp.where(place == aims, weight, 0.0)
 
     at_wall = lax.div(n_norm - normal, n_norm)
-    wall_peers = 4 + (len(y_at) - 1 - len(set(beside_y))) + (zs - 1) + cores * (n_norm - 1)
+    wall_peers = 4 + cores * (zs - 1) + (len(y_at) * n_norm - 1 - len(set(beside_y)))
     pl.semaphore_wait(barrier, 6 + at_wall * wall_peers)
 
     @pl.when(normal == 0)
@@ -636,7 +636,7 @@
     def _():
         for one in wide:
             one.wait_recv()
-        loads_a[y_own] = wall_loads(
+        loads_a[col] = wall_loads(
             span,
             n_span,
             wall_packed,
@@ -648,12 +648,10 @@
             faces,
             jac,
         )
-        for k in y_far:
-            group_copy(loads_a, y_own, 0, device(y_at[k], z, core, 0)).start()
-        take(loads_a.at[1:], 1)
-        loads_b[z] = added(loads_a)
-        for k in z_far:
-            group_copy(loads_b, z, 1, device(here, z_at[k], core, 0)).start()
+        for k in z_far + [0]:
+            for c in range(cores):
+                if k or c:
+                    group_copy(loads_a, col, 0, device(here, z_at[k], core_at[c], 0)).start()
 
     for one in first:
         one.wait_recv()
@@ -696,13 +694,12 @@
 
     @pl.when(normal == 0)
     def _():
-        if zs > 1:
-            take(loads_b.at[1:], 3)
-        loads_c[core] = added(loads_b)
+        take(loads_a.at[1:], 1)
+        loads_b[y_own] = added(loads_a)
         for x in sorted(range(n_norm), key=lambda x: -ring(x, n_norm)):
-            for k in range(cores):
+            for k in y_far + [0]:
                 if x or k:
-                    group_copy(loads_c, core, 2, device(here, z, core_at[k], x)).start()
+                    group_copy(loads_b, y_own, 1, device(y_at[k], z, core, x)).start()
 
     def second_plane(s, carry):
         cells, rates = plane_rates(field2, s, jac)
@@ -770,19 +767,17 @@
         for one in wide:
             one.wait_send()
         take(loads_a.at[1:], 0)
-        if zs > 1:
-            take(loads_b.at[1:], 2)
-        take(tally, 4)
+        take(tally, 2)
 
     @pl.when(normal == 0)
     def _():
-        take(loads_c.at[1:], 5)
+        take(loads_b.at[1:], 3)
 
     @pl.when(normal != 0)
     def _():
-        take(loads_c, 5)
-
-    loads = added(loads_c)
+        take(loads_b, 3)
+
+    loads = added(loads_b)
 
     le, lo = halves(loads)
     fe, fo = fe + le, fo + lo
@@ -855,10 +850,9 @@
                 pltpu.VMEM((1, STATIONS), jnp.int32),
                 pltpu.VMEM((5, 1, STATIONS), f32),
                 pltpu.SMEM((VARS, 3, VARS), f32),
+                pltpu.VMEM((2 * zs, 1, LANES), f32),
                 pltpu.VMEM((ys, 1, LANES), f32),
-                pltpu.VMEM((zs, 1, LANES), f32),
-                pltpu.VMEM((2, 1, LANES), f32),
-                pltpu.VMEM((2 * n_norm - 1, 1, LANES), f32),
+                pltpu.VMEM((ys * n_norm - 1, 1, LANES), f32),
                 pltpu.VMEM((VARS + 1, WRAP, LANES), f32),
                 pltpu.VMEM((3, WRAP, LANES), f32),
                 pltpu.VMEM((2, 3, WRAP, LANES), f32),
@@ -871,7 +865,7 @@
                 pltpu.SemaphoreType.DMA((11,)),
                 pltpu.SemaphoreType.DMA((12,)),
                 pltpu.SemaphoreType.DMA((12,)),
-                pltpu.SemaphoreType.DMA((6,)),
+                pltpu.SemaphoreType.DMA((4,)),
                 pltpu.SemaphoreType.DMA((8,)),
                 pltpu.SemaphoreType.DMA((8,)),
             ],

time: 33.1 us -> 32.6 us (0.985); the launches traced: 32.4 us -> 32.4 us
  no operation moved by 1% of the time
where the time goes in v7:
time: 32.6 us; the launch traced here: 32.4 us
  Pallas kernels  31.8 us (98%)
  between operations  0.64 us (2%)
    pallas_call x1, Pallas kernels, step(): pl.pallas_call(functools.partial(kernel, n_span, n_wrap, n_norm), out_sha...  31 us
    pallas_call x1, Pallas kernels, step(): pl.pallas_call(hand_out, out_shape=(jax.ShapeDtypeStruct(flow_state.shape...  0.75 us

profile of v7, /device:TPU:1, one launch (start us, length us, event | category | flops | bytes accessed | tf_op | source)
XLA Modules:
  0.0 32.4 jit_solution(15244902087796705038)
XLA Ops:
  0.6 31.0 %shard_map.122 = (f32[5,8,16,128]{3,2,1,0:T(8,128)S(1)}, f32[1,128]{1,0:T(1,128)S(1)}) custom-call(f32[5,8,16,128]{3,2,1,0:T(8,128)} %flow_hbm.1, f32[8,16,128]{2,1,0:T(8,128)} %volume_hbm.1, f32[5,3,5]{2,1,0:T(4,128)} %bitcast.8, f32[8,16]{1,0:T(8,128)} %area_hbm.1, s32[8,16]{1,0:T(8,128)} %map_hbm.1, s32[1,128]{1,0:T(1,128)} %bitcast.9, ...), custom_call_target="tpu_custom_call" | custom-call | flops 10000000 | bytes 1000000 | tf_op jit(solution)/shard_map/pallas_call | solution.py:829
  31.7 0.7 %shard_map.123 = (f32[5,8,16,128]{3,2,1,0:T(8,128)}, f32[1,128]{1,0:T(1,128)}) custom-call(f32[5,8,16,128]{3,2,1,0:T(8,128)S(1)} %get-tuple-element.6.flow_ref, f32[1,128]{1,0:T(1,128)S(1)} %get-tuple-element.7.defl_ref), custom_call_target="tpu_custom_call" | custom-call | tf_op jit(solution)/shard_map/pallas_call | solution.py:879

commit v8 on v7

--- a/solution.py
+++ b/solution.py
@@ -11,6 +11,7 @@
 VARS = 5
 STATIONS = 128
 NEWTON = 3
+LEVELS = 6
 DT_FLOW = 0.2
 DISSIPATION = 0.03
 DT_BEAM = 0.2
@@ -160,6 +161,10 @@
     return cells, rates
 
 
+def in_pairs(plane):
+    return lambda i, carry: plane(2 * i + 1, plane(2 * i, carry))
+
+
 def ghost_rates(direction, low, first, second, jac, shape):
     outer, inner = [], []
     for v in range(VARS):
@@ -369,6 +374,7 @@
     contact_v,
     beam_v,
     jac_held,
+    beam_held,
     loads_a,
     loads_b,
     tally,
@@ -566,9 +572,34 @@
                     scaled = jac_held[u, d, v] * (-1.0 / 12.0)
                     jac[25 * d + 5 * u + v] = jnp.full((8, LANES), scaled, jnp.float32)
 
+    def prepare_beam():
+        def permuted(x):
+            full = jnp.broadcast_to(x, (8, LANES))
+            return jnp.take_along_axis(full, held, axis=1)[0:1]
+
+        bending, mass, hardening, disp, vel = [permuted(beam_v[i]) for i in range(5)]
+        contact = permuted(contact_v[...])
+        inertia = 2.0 * mass / (DT_BEAM * DT_BEAM)
+        pull = CONTACT_STIFF * STOP_GAP
+        push = jnp.where(contact == 1, pull, jnp.where(contact == 2, -pull, 0.0))
+        steady = inertia * (disp + DT_BEAM * vel) + push
+        base = inertia + jnp.where(contact > 0, CONTACT_STIFF, 0.0)
+        be, bo = halves(bending)
+        he, ho = halves(hardening)
+        ge, go = halves(base)
+        ue, uo = halves(disp)
+        fe, fo = halves(steady)
+        factors = factor(be, bo, ge + 3.0 * he * ue * ue, go + 3.0 * ho * uo * uo)
+        levels, last = factors
+        kept = [x for level in levels for x in level[1:]] + list(last)
+        kept += [be, bo, ge, go, he, ho, ue, uo, fe, fo]
+        for i, x in enumerate(kept):
+            beam_held[i] = x
+
     @pl.when(normal == 0)
     def _():
         prepare()
+        prepare_beam()
         row_id = lax.broadcasted_iota(jnp.int32, (WRAP, WRAP), 0)
         same = (row_id == lane_of((WRAP, WRAP))).astype(jnp.float32)
 
@@ -595,11 +626,11 @@
             one.start()
 
     first = stage_copies(0, field1)
-    for one in first:
-        one.start()
 
     @pl.when(normal != 0)
     def _():
+        for one in first:
+            one.start()
         prepare()
 
 
@@ -630,10 +661,12 @@
             field2[u, s + 2, TOP : TOP + WRAP, :] = mid.reshape(WRAP, LANES)
         return carry
 
-    lax.fori_loop(0, SPAN, first_plane, 0)
+    lax.fori_loop(0, SPAN // 2, in_pairs(first_plane), 0)
 
     @pl.when(normal == 0)
     def _():
+        for one in first:
+            one.start()
         for one in wide:
             one.wait_recv()
         loads_a[col] = wall_loads(
@@ -692,8 +725,17 @@
         one.start()
 
 
+    @pl.when(normal != 0)
+    def _():
+        prepare_beam()
+
+    for one in first:
+        one.wait_send()
+
     @pl.when(normal == 0)
     def _():
+        for one in wide:
+            one.wait_send()
         take(loads_a.at[1:], 1)
         loads_b[y_own] = added(loads_a)
         for x in sorted(range(n_norm), key=lambda x: -ring(x, n_norm)):
@@ -710,25 +752,7 @@
             result[u, s] = after.reshape(WRAP, LANES)
         return carry
 
-    lax.fori_loop(0, SPAN, second_plane, 0)
-
-    def permuted(x):
-        full = jnp.broadcast_to(x, (8, LANES))
-        return jnp.take_along_axis(full, held, axis=1)[0:1]
-
-    bending, mass, hardening, disp, vel = [permuted(beam_v[i]) for i in range(5)]
-    contact = permuted(contact_v[...])
-    inertia = 2.0 * mass / (DT_BEAM * DT_BEAM)
-    pull = CONTACT_STIFF * STOP_GAP
-    push = jnp.where(contact == 1, pull, jnp.where(contact == 2, -pull, 0.0))
-    steady = inertia * (disp + DT_BEAM * vel) + push
-    base = inertia + jnp.where(contact > 0, CONTACT_STIFF, 0.0)
-    be, bo = halves(bending)
-    he, ho = halves(hardening)
-    ge, go = halves(base)
-    ue, uo = halves(disp)
-    fe, fo = halves(steady)
-    factors = factor(be, bo, ge + 3.0 * he * ue * ue, go + 3.0 * ho * uo * uo)
+    lax.fori_loop(0, SPAN // 2, in_pairs(second_plane), 0)
 
     for one in second:
         one.wait_recv()
@@ -759,13 +783,11 @@
     )
     lax.fori_loop(0, SPAN, columns, 0, unroll=True)
 
-    for one in first + second:
+    for one in second:
         one.wait_send()
 
     @pl.when(normal == 0)
     def _():
-        for one in wide:
-            one.wait_send()
         take(loads_a.at[1:], 0)
         take(tally, 2)
 
@@ -778,7 +800,10 @@
         take(loads_b, 3)
 
     loads = added(loads_b)
-
+    kept = [beam_held[i] for i in range(9 * LEVELS + 14)]
+    levels = [(2**i, *kept[9 * i : 9 * i + 9]) for i in range(LEVELS)]
+    factors = (levels, tuple(kept[9 * LEVELS : 9 * LEVELS + 4]))
+    be, bo, ge, go, he, ho, ue, uo, fe, fo = kept[9 * LEVELS + 4 :]
     le, lo = halves(loads)
     fe, fo = fe + le, fo + lo
     for newton_step in range(NEWTON):
@@ -850,6 +875,7 @@
                 pltpu.VMEM((1, STATIONS), jnp.int32),
                 pltpu.VMEM((5, 1, STATIONS), f32),
                 pltpu.SMEM((VARS, 3, VARS), f32),
+                pltpu.VMEM((9 * LEVELS + 14, 1, LANES), f32),
                 pltpu.VMEM((2 * zs, 1, LANES), f32),
                 pltpu.VMEM((ys, 1, LANES), f32),
                 pltpu.VMEM((ys * n_norm - 1, 1, LANES), f32),

time: 32.6 us -> 31.9 us (0.979)
  Pallas kernels: 31.8 us -> 31.1 us
    pallas_call x1, Pallas kernels: 31 us -> 30.4 us  [step(): pl.pallas_call(functools.partial(kernel, n_span, n_wrap, n_norm), out_sha...]
where the time goes in v8:
time: 31.9 us; the launch traced here: 31.8 us
  Pallas kernels  31.1 us (97%)
  between operations  0.64 us (2%)
    pallas_call x1, Pallas kernels, step(): pl.pallas_call(functools.partial(kernel, n_span, n_wrap, n_norm), out_sha...  30.4 us
    pallas_call x1, Pallas kernels, step(): pl.pallas_call(hand_out, out_shape=(jax.ShapeDtypeStruct(flow_state.shape...  0.75 us

profile of v8, /device:TPU:1, one launch (start us, length us, event | category | flops | bytes accessed | tf_op | source)
XLA Modules:
  0.0 31.8 jit_solution(7202071513460239061)
XLA Ops:
  0.6 30.4 %shard_map.122 = (f32[5,8,16,128]{3,2,1,0:T(8,128)S(1)}, f32[1,128]{1,0:T(1,128)S(1)}) custom-call(f32[5,8,16,128]{3,2,1,0:T(8,128)} %flow_hbm.1, f32[8,16,128]{2,1,0:T(8,128)} %volume_hbm.1, f32[5,3,5]{2,1,0:T(4,128)} %bitcast.8, f32[8,16]{1,0:T(8,128)} %area_hbm.1, s32[8,16]{1,0:T(8,128)} %map_hbm.1, s32[1,128]{1,0:T(1,128)} %bitcast.9, ...), custom_call_target="tpu_custom_call" | custom-call | flops 10000000 | bytes 1000000 | tf_op jit(solution)/shard_map/pallas_call | solution.py:854
  31.0 0.7 %shard_map.123 = (f32[5,8,16,128]{3,2,1,0:T(8,128)}, f32[1,128]{1,0:T(1,128)}) custom-call(f32[5,8,16,128]{3,2,1,0:T(8,128)S(1)} %get-tuple-element.6.flow_ref, f32[1,128]{1,0:T(1,128)S(1)} %get-tuple-element.7.defl_ref), custom_call_target="tpu_custom_call" | custom-call | tf_op jit(solution)/shard_map/pallas_call | solution.py:905

commit v9 on v8

--- a/solution.py
+++ b/solution.py
@@ -161,8 +161,13 @@
     return cells, rates
 
 
-def in_pairs(plane):
-    return lambda i, carry: plane(2 * i + 1, plane(2 * i, carry))
+def in_fours(plane):
+    def four(i, carry):
+        for j in range(4):
+            carry = plane(4 * i + j, carry)
+        return carry
+
+    return four
 
 
 def ghost_rates(direction, low, first, second, jac, shape):
@@ -627,10 +632,11 @@
 
     first = stage_copies(0, field1)
 
+    for one in first:
+        one.start()
+
     @pl.when(normal != 0)
     def _():
-        for one in first:
-            one.start()
         prepare()
 
 
@@ -661,12 +667,10 @@
             field2[u, s + 2, TOP : TOP + WRAP, :] = mid.reshape(WRAP, LANES)
         return carry
 
-    lax.fori_loop(0, SPAN // 2, in_pairs(first_plane), 0)
+    lax.fori_loop(0, SPAN // 4, in_fours(first_plane), 0)
 
     @pl.when(normal == 0)
     def _():
-        for one in first:
-            one.start()
         for one in wide:
             one.wait_recv()
         loads_a[col] = wall_loads(
@@ -752,7 +756,7 @@
             result[u, s] = after.reshape(WRAP, LANES)
         return carry
 
-    lax.fori_loop(0, SPAN // 2, in_pairs(second_plane), 0)
+    lax.fori_loop(0, SPAN // 4, in_fours(second_plane), 0)
 
     for one in second:
         one.wait_recv()

time: 31.9 us -> 32.6 us (1.022)
  Pallas kernels: 31.1 us -> 31.8 us
    pallas_call x1, Pallas kernels: 30.4 us -> 31 us  [step(): pl.pallas_call(functools.partial(kernel, n_span, n_wrap, n_norm), out_sha...]
where the time goes in v9:
time: 32.6 us; the launch traced here: 32.4 us
  Pallas kernels  31.8 us (98%)
  between operations  0.64 us (2%)
    pallas_call x1, Pallas kernels, step(): pl.pallas_call(functools.partial(kernel, n_span, n_wrap, n_norm), out_sha...  31 us
    pallas_call x1, Pallas kernels, step(): pl.pallas_call(hand_out, out_shape=(jax.ShapeDtypeStruct(flow_state.shape...  0.75 us

profile of v9, /device:TPU:1, one launch (start us, length us, event | category | flops | bytes accessed | tf_op | source)
XLA Modules:
  0.0 32.4 jit_solution(12607086816726339121)
XLA Ops:
  0.6 31.0 %shard_map.122 = (f32[5,8,16,128]{3,2,1,0:T(8,128)S(1)}, f32[1,128]{1,0:T(1,128)S(1)}) custom-call(f32[5,8,16,128]{3,2,1,0:T(8,128)} %flow_hbm.1, f32[8,16,128]{2,1,0:T(8,128)} %volume_hbm.1, f32[5,3,5]{2,1,0:T(4,128)} %bitcast.8, f32[8,16]{1,0:T(8,128)} %area_hbm.1, s32[8,16]{1,0:T(8,128)} %map_hbm.1, s32[1,128]{1,0:T(1,128)} %bitcast.9, ...), custom_call_target="tpu_custom_call" | custom-call | flops 10000000 | bytes 1000000 | tf_op jit(solution)/shard_map/pallas_call | solution.py:858
  31.7 0.7 %shard_map.123 = (f32[5,8,16,128]{3,2,1,0:T(8,128)}, f32[1,128]{1,0:T(1,128)}) custom-call(f32[5,8,16,128]{3,2,1,0:T(8,128)S(1)} %get-tuple-element.6.flow_ref, f32[1,128]{1,0:T(1,128)S(1)} %get-tuple-element.7.defl_ref), custom_call_target="tpu_custom_call" | custom-call | tf_op jit(solution)/shard_map/pallas_call | solution.py:909

commit v10 on v9

--- a/solution.py
+++ b/solution.py
@@ -604,22 +604,6 @@
     @pl.when(normal == 0)
     def _():
         prepare()
-        prepare_beam()
-        row_id = lax.broadcasted_iota(jnp.int32, (WRAP, WRAP), 0)
-        same = (row_id == lane_of((WRAP, WRAP))).astype(jnp.float32)
-
-        def turned_over(x):
-            return lax.dot_general(
-                same, x, (((1,), (1,)), ((), ())), precision=lax.Precision.HIGHEST
-            )
-
-        weights = turned_over(area[...])
-        places = turned_over(stations[...].astype(jnp.float32))
-        aims = jnp.broadcast_to(held[0:1], (WRAP, LANES)).astype(jnp.float32)
-        for s in range(SPAN):
-            weight = jnp.broadcast_to(weights[:, s : s + 1], (WRAP, LANES))
-            place = jnp.broadcast_to(places[:, s : s + 1], (WRAP, LANES))
-            faces[s] = jnp.where(place == aims, weight, 0.0)
 
     at_wall = lax.div(n_norm - normal, n_norm)
     wall_peers = 4 + cores * (zs - 1) + (len(y_at) * n_norm - 1 - len(set(beside_y)))
@@ -632,11 +616,10 @@
 
     first = stage_copies(0, field1)
 
-    for one in first:
-        one.start()
-
     @pl.when(normal != 0)
     def _():
+        for one in first:
+            one.start()
         prepare()
 
 
@@ -671,6 +654,23 @@
 
     @pl.when(normal == 0)
     def _():
+        for one in first:
+            one.start()
+        row_id = lax.broadcasted_iota(jnp.int32, (WRAP, WRAP), 0)
+        same = (row_id == lane_of((WRAP, WRAP))).astype(jnp.float32)
+
+        def turned_over(x):
+            return lax.dot_general(
+                same, x, (((1,), (1,)), ((), ())), precision=lax.Precision.HIGHEST
+            )
+
+        weights = turned_over(area[...])
+        places = turned_over(stations[...].astype(jnp.float32))
+        aims = jnp.broadcast_to(held[0:1], (WRAP, LANES)).astype(jnp.float32)
+        for s in range(SPAN):
+            weight = jnp.broadcast_to(weights[:, s : s + 1], (WRAP, LANES))
+            place = jnp.broadcast_to(places[:, s : s + 1], (WRAP, LANES))
+            faces[s] = jnp.where(place == aims, weight, 0.0)
         for one in wide:
             one.wait_recv()
         loads_a[col] = wall_loads(
@@ -729,10 +729,6 @@
         one.start()
 
 
-    @pl.when(normal != 0)
-    def _():
-        prepare_beam()
-
     for one in first:
         one.wait_send()
 
@@ -758,6 +754,7 @@
 
     lax.fori_loop(0, SPAN // 4, in_fours(second_plane), 0)
 
+    prepare_beam()
     for one in second:
         one.wait_recv()
     stage_columns(1)

time: 32.6 us -> 32 us (0.982)
  Pallas kernels: 31.8 us -> 31.1 us
    pallas_call x1, Pallas kernels: 31 us -> 30.4 us  [step(): pl.pallas_call(functools.partial(kernel, n_span, n_wrap, n_norm), out_sha...]
where the time goes in v10:
time: 32 us; the launch traced here: 31.8 us
  Pallas kernels  31.1 us (97%)
  between operations  0.64 us (2%)
    pallas_call x1, Pallas kernels, step(): pl.pallas_call(functools.partial(kernel, n_span, n_wrap, n_norm), out_sha...  30.4 us
    pallas_call x1, Pallas kernels, step(): pl.pallas_call(hand_out, out_shape=(jax.ShapeDtypeStruct(flow_state.shape...  0.75 us

profile of v10, /device:TPU:1, one launch (start us, length us, event | category | flops | bytes accessed | tf_op | source)
XLA Modules:
  0.0 31.8 jit_solution(2450313198446307160)
XLA Ops:
  0.6 30.4 %shard_map.122 = (f32[5,8,16,128]{3,2,1,0:T(8,128)S(1)}, f32[1,128]{1,0:T(1,128)S(1)}) custom-call(f32[5,8,16,128]{3,2,1,0:T(8,128)} %flow_hbm.1, f32[8,16,128]{2,1,0:T(8,128)} %volume_hbm.1, f32[5,3,5]{2,1,0:T(4,128)} %bitcast.8, f32[8,16]{1,0:T(8,128)} %area_hbm.1, s32[8,16]{1,0:T(8,128)} %map_hbm.1, s32[1,128]{1,0:T(1,128)} %bitcast.9, ...), custom_call_target="tpu_custom_call" | custom-call | flops 10000000 | bytes 1000000 | tf_op jit(solution)/shard_map/pallas_call | solution.py:855
  31.0 0.7 %shard_map.123 = (f32[5,8,16,128]{3,2,1,0:T(8,128)}, f32[1,128]{1,0:T(1,128)}) custom-call(f32[5,8,16,128]{3,2,1,0:T(8,128)S(1)} %get-tuple-element.6.flow_ref, f32[1,128]{1,0:T(1,128)S(1)} %get-tuple-element.7.defl_ref), custom_call_target="tpu_custom_call" | custom-call | tf_op jit(solution)/shard_map/pallas_call | solution.py:906

commit v11 on v8

--- a/solution.py
+++ b/solution.py
@@ -627,9 +627,12 @@
 
     first = stage_copies(0, field1)
 
+    for one in first[:2] + first[4:]:
+        one.start()
+
     @pl.when(normal != 0)
     def _():
-        for one in first:
+        for one in first[2:4]:
             one.start()
         prepare()
 
@@ -665,7 +668,7 @@
 
     @pl.when(normal == 0)
     def _():
-        for one in first:
+        for one in first[2:4]:
             one.start()
         for one in wide:
             one.wait_recv()

time: 31.9 us -> 32.4 us (1.016)
  Pallas kernels: 31.1 us -> 31.6 us
    pallas_call x1, Pallas kernels: 30.4 us -> 30.8 us  [step(): pl.pallas_call(functools.partial(kernel, n_span, n_wrap, n_norm), out_sha...]
where the time goes in v11:
time: 32.4 us; the launch traced here: 32.2 us
  Pallas kernels  31.6 us (98%)
  between operations  0.64 us (2%)
    pallas_call x1, Pallas kernels, step(): pl.pallas_call(functools.partial(kernel, n_span, n_wrap, n_norm), out_sha...  30.8 us
    pallas_call x1, Pallas kernels, step(): pl.pallas_call(hand_out, out_shape=(jax.ShapeDtypeStruct(flow_state.shape...  0.75 us

profile of v11, /device:TPU:1, one launch (start us, length us, event | category | flops | bytes accessed | tf_op | source)
XLA Modules:
  0.0 32.2 jit_solution(16642290604868812613)
XLA Ops:
  0.6 30.8 %shard_map.122 = (f32[5,8,16,128]{3,2,1,0:T(8,128)S(1)}, f32[1,128]{1,0:T(1,128)S(1)}) custom-call(f32[5,8,16,128]{3,2,1,0:T(8,128)} %flow_hbm.1, f32[8,16,128]{2,1,0:T(8,128)} %volume_hbm.1, f32[5,3,5]{2,1,0:T(4,128)} %bitcast.8, f32[8,16]{1,0:T(8,128)} %area_hbm.1, s32[8,16]{1,0:T(8,128)} %map_hbm.1, s32[1,128]{1,0:T(1,128)} %bitcast.9, ...), custom_call_target="tpu_custom_call" | custom-call | flops 10000000 | bytes 1000000 | tf_op jit(solution)/shard_map/pallas_call | solution.py:857
  31.5 0.7 %shard_map.123 = (f32[5,8,16,128]{3,2,1,0:T(8,128)}, f32[1,128]{1,0:T(1,128)}) custom-call(f32[5,8,16,128]{3,2,1,0:T(8,128)S(1)} %get-tuple-element.6.flow_ref, f32[1,128]{1,0:T(1,128)S(1)} %get-tuple-element.7.defl_ref), custom_call_target="tpu_custom_call" | custom-call | tf_op jit(solution)/shard_map/pallas_call | solution.py:908
